TPU v7x, 128 devices: a whole 4x4x4 slice. The times are simulated.
128 devices in a mesh: seq: 64 (over z, y, x), mp: 2 (over core).
Axes of the slice: x: 4, y: 4, z: 4, core: 2. Of those that a mesh axis runs over, the one named last changes fastest.
Arguments:
- tokens: bfloat16 [16384, 1024], P('seq')
- token_sizes: int32 [16384], P('seq'), may hold values from 1 to 8
- merge_source: int32 [64, 128], P('seq'), may hold values from 0 to 127, each once within a row
- merge_target: int32 [64, 128], P('seq'), may hold values from 0 to 127
- merge_count: int32 [64], P('seq'), may hold values from 0 to 128, as said below
- attn_gain: float32 [1024], replicated, may hold values from 0.25 to 1.75
- qkv_weight: bfloat16 [3, 1024, 1024], P(None, None, 'mp')
- out_weight: bfloat16 [1024, 1024], P('mp'), may hold values from -0.1875 to 0.1875
- mlp_gain: float32 [1024], replicated, may hold values from 0.25 to 1.75
- up_weight: bfloat16 [1024, 4096], P(None, 'mp'), may hold values from -0.1875 to 0.1875
- down_weight: bfloat16 [4096, 1024], P('mp'), may hold values from -0.09375 to 0.09375
Outputs:
- merged_out: bfloat16 [16384, 1024], P('seq')
- best_score: float32 [8192], P('seq')
Inputs may be any that keep to these rules, and one draw needn't show every extreme that they name: `merge_count`: one shard makes 128 merges and another none, in every draw.
All inputs are finite; a program needn't handle non-finite values.
Results may differ from a plain program's by a relative error of at most 0.007.
Values may be sent and summed in bfloat16 or wider, within the bound.
A program may use at most 384 MiB of HBM per device.

v0:
```python
import jax
import jax.numpy as jnp
from jax import lax
from jax.sharding import PartitionSpec as P

HEAD_DIM = 64


epsilon = 1e-06
empty_bias = -10000.0


def from_behind(shard, axis, by):
    devices = lax.axis_size(axis)
    return lax.ppermute(shard, axis, [(i, (i + by) % devices) for i in range(devices)])


def layer_norm(values, gain_vector):
    center = values - jnp.mean(values, axis=-1, keepdims=True)
    spread = jnp.mean(center * center, axis=-1, keepdims=True)
    return center * lax.rsqrt(spread + epsilon) * gain_vector


def project(inputs, weight):
    return jnp.dot(inputs, weight, preferred_element_type=jnp.float32).astype(jnp.bfloat16)


def on_device(
    tokens,
    token_sizes,
    merge_source,
    merge_target,
    merge_count,
    attn_gain,
    qkv_weight,
    out_weight,
    mlp_gain,
    up_weight,
    down_weight,
):
    shard_count = lax.axis_size("seq")
    my_index = lax.axis_index("seq")
    row_count = tokens.shape[0]
    half_rows = row_count // 2
    model_width = tokens.shape[1]
    slot_rows = row_count // shard_count
    local_width = qkv_weight.shape[2]
    head_count = local_width // HEAD_DIM
    normed = layer_norm(tokens.astype(jnp.float32), attn_gain).astype(jnp.bfloat16)
    metric = project(normed, qkv_weight[1])
    partner = from_behind(metric[:half_rows], "seq", -1)
    own_keys = metric[half_rows:]
    products = lax.dot_general(
        own_keys, partner, (((1,), (1,)), ((), ())), preferred_element_type=jnp.float32
    )
    own_square = jnp.sum(jnp.square(own_keys.astype(jnp.float32)), axis=1)
    partner_square = jnp.sum(jnp.square(partner.astype(jnp.float32)), axis=1)
    products, own_square, partner_square = lax.psum((products, own_square, partner_square), "mp")
    cosine = (
        products
        * lax.rsqrt(own_square + epsilon)[:, None]
        * lax.rsqrt(partner_square + epsilon)[None, :]
    )
    best_score = jnp.max(cosine, axis=1)
    partner_ids = jnp.arange(half_rows, dtype=jnp.int32)
    active = partner_ids < merge_count[0]
    source = merge_source[0]
    target = merge_target[0]
    source_size = jnp.where(active, token_sizes[half_rows + source], 0).astype(jnp.float32)
    weights = (
        (target[None, :] == partner_ids[:, None]).astype(jnp.float32) * source_size[None, :]
    ).astype(jnp.bfloat16)
    picked = tokens[half_rows + source]
    added_rows = jnp.dot(weights, picked, preferred_element_type=jnp.float32)
    added_size = jnp.sum(weights.astype(jnp.float32), axis=1)
    added_rows, added_size = from_behind((added_rows, added_size), "seq", 1)
    base_size = token_sizes[:half_rows].astype(jnp.float32)
    merged = (base_size[:, None] * tokens[:half_rows].astype(jnp.float32) + added_rows) / (
        base_size + added_size
    )[:, None]
    new_rows = jnp.concatenate([merged.astype(jnp.bfloat16), tokens[half_rows:]], axis=0)
    new_size = jnp.concatenate(
        [base_size + added_size, token_sizes[half_rows:].astype(jnp.float32)]
    )
    removed = jnp.any((source[:, None] == partner_ids[None, :]) & active[:, None], axis=0)
    survive = jnp.concatenate([jnp.ones((half_rows,), bool), jnp.logical_not(removed)])
    keep_int = survive.astype(jnp.int32)
    local_rank = jnp.cumsum(keep_int) - 1
    kept_total = jnp.sum(keep_int)
    all_counts = lax.all_gather(kept_total.reshape(1), "seq", axis=0, tiled=True)
    before = jnp.cumsum(all_counts) - all_counts
    shard_ids = jnp.arange(shard_count, dtype=jnp.int32)
    my_start = jnp.sum(jnp.where(shard_ids == my_index, before, 0))
    grand_total = jnp.sum(all_counts)
    global_rank = my_start + local_rank
    flat_slot = global_rank % shard_count * slot_rows + local_rank // shard_count
    flat_slot = jnp.where(survive, flat_slot, row_count)
    wanted = jnp.arange(row_count, dtype=jnp.int32) * shard_count + my_index
    filled = wanted < grand_total
    sender = jnp.sum((before[None, :] <= wanted[:, None]).astype(jnp.int32), axis=1) - 1
    sender_start = jnp.sum(
        jnp.where(sender[:, None] == shard_ids[None, :], before[None, :], 0), axis=1
    )
    fetch_index = sender * slot_rows + (wanted - sender_start) // shard_count
    fetch_index = jnp.where(filled, fetch_index, 0)
    outgoing = (
        jnp.zeros((row_count, model_width), jnp.bfloat16).at[flat_slot].set(new_rows, mode="drop")
    )
    outgoing = outgoing.reshape(shard_count, slot_rows, model_width)
    empty_value = jnp.asarray(empty_bias, jnp.float32).astype(jnp.bfloat16)
    bias_rows = jnp.log(new_size).astype(jnp.bfloat16)
    outgoing_bias = (
        jnp.full((row_count,), empty_bias, jnp.float32)
        .astype(jnp.bfloat16)
        .at[flat_slot]
        .set(bias_rows, mode="drop")
    )
    outgoing_bias = outgoing_bias.reshape(shard_count, slot_rows)
    arrived, arrived_bias = (
        lax.all_to_all(outgoing, "seq", split_axis=0, concat_axis=0, tiled=True),
        lax.all_to_all(outgoing_bias, "seq", split_axis=0, concat_axis=0, tiled=True),
    )
    balanced = jnp.where(
        filled[:, None],
        arrived.reshape(row_count, model_width)[fetch_index],
        jnp.zeros((), jnp.bfloat16),
    )
    key_bias = jnp.where(filled, arrived_bias.reshape(row_count)[fetch_index], empty_value)
    normed_bal = layer_norm(balanced.astype(jnp.float32), attn_gain).astype(jnp.bfloat16)
    queries = project(normed_bal, qkv_weight[0])
    key_block = project(normed_bal, qkv_weight[1])
    value_block = project(normed_bal, qkv_weight[2])
    score_scale = HEAD_DIM ** (-0.5)
    query_heads = queries.reshape(row_count, head_count, HEAD_DIM)
    row_peak = jnp.full((head_count, row_count), -1e30, jnp.float32)
    piece_keys = lax.all_gather(key_block, "seq", axis=0, tiled=True)
    piece_values = lax.all_gather(value_block, "seq", axis=0, tiled=True)
    piece_bias = lax.all_gather(key_bias, "seq", axis=0, tiled=True)
    length = piece_keys.shape[0]
    key_heads = piece_keys.reshape(length, head_count, HEAD_DIM)
    value_heads = piece_values.reshape(length, head_count, HEAD_DIM)
    scores = (
        jnp.einsum("qhd,khd->hqk", query_heads, key_heads, preferred_element_type=jnp.float32)
        * score_scale
    )
    scores = scores + piece_bias.astype(jnp.float32)[None, None, :]
    new_peak = jnp.maximum(row_peak, jnp.max(scores, axis=2))
    exponent = jnp.exp(scores - new_peak[:, :, None])
    total_weight = jnp.sum(exponent, axis=2)
    weighted_sum = jnp.einsum(
        "hqk,khd->hqd",
        exponent.astype(jnp.bfloat16),
        value_heads,
        preferred_element_type=jnp.float32,
    )
    row_peak, total_weight, weighted_sum = (new_peak, total_weight, weighted_sum)
    mixed = (
        (weighted_sum / total_weight[:, :, None])
        .transpose(1, 0, 2)
        .reshape(row_count, local_width)
        .astype(jnp.bfloat16)
    )
    attention = lax.psum(jnp.dot(mixed, out_weight, preferred_element_type=jnp.float32), "mp")
    layer_one = (balanced.astype(jnp.float32) + attention).astype(jnp.bfloat16)
    normed_mlp = layer_norm(layer_one.astype(jnp.float32), mlp_gain).astype(jnp.bfloat16)
    hidden = jax.nn.gelu(
        jnp.dot(normed_mlp, up_weight, preferred_element_type=jnp.float32), approximate=False
    ).astype(jnp.bfloat16)
    result = layer_one.astype(jnp.float32) + lax.psum(
        jnp.dot(hidden, down_weight, preferred_element_type=jnp.float32), "mp"
    )
    merged_out = jnp.where(filled[:, None], result, 0.0).astype(jnp.bfloat16)
    return (merged_out, best_score)


def solution(mesh):
    placed = (
        P("seq", None),
        P("seq"),
        P("seq", None),
        P("seq", None),
        P("seq"),
        P(),
        P(None, None, "mp"),
        P("mp", None),
        P(),
        P(None, "mp"),
        P("mp", None),
    )
    return jax.shard_map(
        on_device, mesh=mesh, in_specs=placed, out_specs=(P("seq", None), P("seq")), check_vma=False
    )
```

profile of v0, /device:TPU:1, one launch (start us, length us, event | category | flops | bytes accessed | tf_op | source)
XLA Modules:
  0.0 522.0 jit_solution(4594012467065019146)
XLA Ops:
  11.1 2.1 collective-permute-start.1
  13.2 2.2 gather_fusion.1
  20.5 23.4 %all-reduce.1 = s32[64]{0:T(128)S(1)} all-reduce(s32[64]{0:T(128)S(1)} %dynamic-update-slice), channel_id=1, replica_groups=mesh['seq'=64,'mp'=2] {'seq'}, use_global_device_ids=true, to_apply=%add.1 | all-reduce | flops 64 | bytes 512
  46.4 2.2 scatter_custom_fusion.1
  49.3 5.4 %all-to-all-start.1 = ((bf16[64,1,4]{2,1,0:T(2,128)(2,1)}), bf16[64,1,4]{2,1,0:T(2,128)(2,1)S(1)}, u32[]{:S(2)}, u32[]{:S(2)}) async-start(bf16[64,1,4]{2,1,0:T(2,128)(2,1)} %all_to_all.12), calls=%async_computation.1 | async-start | bytes 65536 | tf_op jit(solution)/shard_map/all_to_all | solution.py:121
  54.8 1.8 scatter_custom_fusion
  57.6 5.4 %all-to-all-done.1 = bf16[64,1,4]{2,1,0:T(2,128)(2,1)S(1)} async-done(((bf16[64,1,4]{2,1,0:T(2,128)(2,1)}), bf16[64,1,4]{2,1,0:T(2,128)(2,1)S(1)}, u32[]{:S(2)}, u32[]{:S(2)}) %all-to-all-start.1) | async-done | bytes 544 | tf_op jit(solution)/shard_map/all_to_all | solution.py:121
  63.0 4.7 all-to-all-start
  68.6 1.9 gather_fusion.3
  71.2 7.4 %all-to-all-done = bf16[64,4,1024]{2,1,0:T(4,128)(2,1)S(1)} async-done(((bf16[64,4,1024]{2,1,0:T(4,128)(2,1)}), bf16[64,4,1024]{2,1,0:T(4,128)(2,1)S(1)}, u32[]{:S(2)}, u32[]{:S(2)}) %all-to-all-start) | async-done | bytes 524320 | tf_op jit(solution)/shard_map/all_to_all | solution.py:120
  80.4 2.5 convolution_convert_fusion.2
  83.0 2.5 convolution_convert_fusion.1
  85.7 143.5 %all-gather = bf16[64,1,256]{2,1,0:T(2,128)(2,1)S(1)} all-gather(bf16[1,1,256]{2,1,0:T(2,128)(2,1)S(1)} %reshape.328), channel_id=1, replica_groups=mesh['seq'=64,'mp'=2] {'seq'}, dimensions={0}, use_global_device_ids=true | all-gather | bytes 33280 | tf_op jit(solution)/shard_map/all_gather | solution.py:138
  231.1 21.6 %copy.28 = bf16[16384,512]{0,1:T(8,128)(2,1)} copy(bf16[16384,512]{1,0:T(8,128)(2,1)} %all-gather.4.cloned.1.call-done) | data formatting | bytes 33554432 | tf_op jit(solution)/shard_map/all_gather | solution.py:136
  252.7 53.1 %fusion = (f32[8,256]{1,0:T(8,128)S(1)}, f32[8,256,16384]{2,1,0:T(8,128)}) fusion(f32[16384]{0:T(1024)S(1)} %bitcast.68, bf16[256,8,64]{0,2,1:T(8,128)(2,1)S(1)} %bitcast.71, bf16[16384,8,64]{0,2,1:T(8,128)(2,1)} %bitcast.66), kind=kOutput, calls=%fused_computation.8 | convolution fusion | flops 4395628544 | bytes 151330816 | tf_op jit(solution)/shard_map/qhd,khd->hqk/dot_general | solution.py:143
  305.8 41.2 %fusion.1 = f32[8,256]{1,0:T(8,128)S(1)} fusion(f32[8,256,16384]{2,1,0:T(8,128)} %get-tuple-element.18, f32[8,256]{1,0:T(8,128)S(1)} %broadcast_maximum_fusion, f32[16384]{0:T(1024)S(1)} %bitcast.69), kind=kLoop, calls=%fused_computation.9 | loop fusion | flops 134215680 | bytes 134299648 | tf_op jit(solution)/shard_map/reduce_sum | solution.py:149
  347.0 21.3 %copy.30 = bf16[16384,512]{0,1:T(8,128)(2,1)} copy(bf16[16384,512]{1,0:T(8,128)(2,1)} %all-gather.6.cloned.1.call-done) | data formatting | bytes 33554432 | tf_op jit(solution)/shard_map/all_gather | solution.py:137
  368.3 48.7 %fusion.27 = bf16[256,8,64]{0,2,1:T(8,128)(2,1)S(1)} fusion(bf16[16384,8,64]{0,2,1:T(8,128)(2,1)} %bitcast.67, f32[8,256,16384]{2,1,0:T(8,128)} %get-tuple-element.18, f32[8,256]{1,0:T(8,128)S(1)} %broadcast_maximum_fusion, f32[16384]{0:T(1024)S(1)} %bitcast.70, f32[256,8]{0,1:T(8,128)S(1)} %bitcast.73), kind=kOutput, calls=%fused_computation.51 | convolution fusion | flops 4429447168 | bytes 151339008 | tf_op jit(solution)/shard_map/hqk,khd->hqd/dot_general | solution.py:150
  421.7 3.0 collective-permute-done.2
  425.6 47.1 %all-reduce.7.cloned.1.call-done = f32[256,1024]{1,0:T(8,128)} async-done(((f32[256,1024]{1,0:T(8,128)}), f32[256,1024]{1,0:T(8,128)}) %all-reduce.7.cloned.1.call-update) | async-done | bytes 1048592 | tf_op jit(solution)/shard_map/psum | solution.py:163
  474.5 11.1 %fusion.30 = f32[256,1024]{1,0:T(8,128)} fusion(bf16[2048,1024]{1,0:T(8,128)(2,1)} %param.21, bf16[1024,2048]{1,0:T(8,128)(2,1)} %param.20, bf16[256,1024]{1,0:T(8,128)(2,1)S(1)} %get-tuple-element.7, f32[1024]{0:T(1024)S(1)} %copy-done.6, f32[256]{0:T(256)S(1)} %add_rsqrt_fusion.1, f32[256]{0:T(256)S(1)} %broadcast_multiply_fusion.1), kind=kOutput, calls=%fused_computation.52 | convolution fusion | flops 2182873088 | bytes 9967616 | tf_op jit(solution)/shard_map/dot_general | solution.py:170
  485.9 2.5 all-reduce.2
  488.4 24.1 %all-reduce.9.cloned.1.call-done = (f32[256,1024]{1,0:T(8,128)}, f32[128,128]{1,0:T(8,128)}) async-done(((f32[256,1024]{1,0:T(8,128)}, f32[128,128]{1,0:T(8,128)}), (f32[256,1024]{1,0:T(8,128)}, f32[128,128]{1,0:T(8,128)})) %all-reduce.9.cloned.1.call-update) | async-done | bytes 1114128 | tf_op jit(solution)/shard_map/psum | solution.py:169
  512.6 2.2 fusion.43
  (99 shorter events, 26.6 us)
Async XLA Ops:
  7.2 409.8 %copy-start = (bf16[512,1024]{1,0:T(8,128)(2,1)S(1)}, bf16[512,1024]{1,0:T(8,128)(2,1)}, u32[]{:S(2)}) copy-start(bf16[512,1024]{1,0:T(8,128)(2,1)} %param.18) | copy-start | bytes 3145732
  7.2 11.2 %copy-start.8 = (u32[128]{0:T(128)S(1)}, u32[128]{0:T(128)}, u32[]{:S(2)}) copy-start(u32[128]{0:T(128)} %constant.160) | copy-start | bytes 1540
  7.2 10.4 %copy-start.7 = (s32[1,128]{1,0:T(1,128)S(1)}, s32[1,128]{1,0:T(1,128)}, u32[]{:S(2)}) copy-start(s32[1,128]{1,0:T(1,128)} %param.13) | copy-start | bytes 1540
  7.2 39.0 %copy-start.1 = (s32[256]{0:T(256)S(1)}, s32[256]{0:T(256)}, u32[]{:S(2)}) copy-start(s32[256]{0:T(256)} %param.12) | copy-start | bytes 3076
  7.2 8.2 %copy-start.4 = (s32[1,128]{1,0:T(1,128)S(1)}, s32[1,128]{1,0:T(1,128)}, u32[]{:S(2)}) copy-start(s32[1,128]{1,0:T(1,128)} %param.14) | copy-start | bytes 1540
  10.3 44.4 %copy-start.2 = (bf16[256,1024]{1,0:T(8,128)(2,1)S(1)}, bf16[256,1024]{1,0:T(8,128)(2,1)}, u32[]{:S(2)}) copy-start(bf16[256,1024]{1,0:T(8,128)(2,1)} %param.11) | copy-start | bytes 1572868
  11.1 43.7 %slice-start = ((bf16[256,1024]{1,0:T(8,128)(2,1)}), bf16[128,1024]{1,0:T(8,128)(2,1)S(1)}, s32[]{:S(2)}) async-start(bf16[256,1024]{1,0:T(8,128)(2,1)} %param.11), calls=%async_computation.6 | async-start | bytes 524288 | tf_op jit(solution)/shard_map/slice | solution.py:81
  11.1 35.2 %collective-permute-start.1 = (f32[128]{0:T(128)S(1)}, f32[128]{0:T(128)S(1)}, u32[]{:S(2)}, u32[]{:S(2)}) collective-permute-start(f32[128]{0:T(128)S(1)} %convert_reduce_fusion.4), channel_id=1, source_target_pairs={{0,2},{2,4},{4,6},{6,8},{8,10},{10,12},{12,14},{14,16},{16,18},{18... | collective-permute-start | bytes 1544 | tf_op jit(solution)/shard_map/ppermute | solution.py:15
  16.4 38.2 %collective-permute-start = (f32[128,1024]{1,0:T(8,128)}, f32[128,1024]{1,0:T(8,128)S(1)}, u32[]{:S(2)}, u32[]{:S(2)}) collective-permute-start(f32[128,1024]{1,0:T(8,128)} %fusion.107), channel_id=1, source_target_pairs={{0,2},{2,4},{4,6},{6,8},{8,10},{10,12},{12,14},{14,16},{16,18},{18... | collective-permute-start | bytes 1572872 | tf_op jit(solution)/shard_map/ppermute | solution.py:15
  49.3 13.8 %all-to-all-start.1 = ((bf16[64,1,4]{2,1,0:T(2,128)(2,1)}), bf16[64,1,4]{2,1,0:T(2,128)(2,1)S(1)}, u32[]{:S(2)}, u32[]{:S(2)}) async-start(bf16[64,1,4]{2,1,0:T(2,128)(2,1)} %all_to_all.12), calls=%async_computation.1 | async-start | bytes 65536 | tf_op jit(solution)/shard_map/all_to_all | solution.py:121
  63.0 15.5 %all-to-all-start = ((bf16[64,4,1024]{2,1,0:T(4,128)(2,1)}), bf16[64,4,1024]{2,1,0:T(4,128)(2,1)S(1)}, u32[]{:S(2)}, u32[]{:S(2)}) async-start(bf16[64,4,1024]{2,1,0:T(4,128)(2,1)} %reshape.269), calls=%async_computation | async-start | bytes 1048576 | tf_op jit(solution)/shard_map/all_to_all | solution.py:120
  67.7 163.4 %all-gather.4.cloned.1.call-start = ((), (), s32[]{:S(2)}) async-start(), calls=%async_computation.2 | async-start | bytes 17039360 | tf_op jit(solution)/shard_map/all_gather | solution.py:136
  78.6 1.8 copy-start.5
  82.9 264.1 %all-gather.6.cloned.1.call-start = ((), (), s32[]{:S(2)}) async-start(), calls=%async_computation.3 | async-start | bytes 17039360 | tf_op jit(solution)/shard_map/all_gather | solution.py:137
  85.5 387.2 %all-reduce.7.cloned.1.call-start = ((), (), s32[]{:S(2)}) async-start(), calls=%async_computation.4 | async-start | bytes 2097152 | tf_op jit(solution)/shard_map/psum | solution.py:163
  418.5 94.0 %all-reduce.9.cloned.1.call-start = ((), (), s32[]{:S(2)}) async-start(), calls=%async_computation.5 | async-start | bytes 2228224 | tf_op jit(solution)/shard_map/psum | solution.py:169
  420.6 53.9 %copy-start.6 = (f32[1024]{0:T(1024)S(1)}, f32[1024]{0:T(1024)}, u32[]{:S(2)}) copy-start(f32[1024]{0:T(1024)} %param.19) | copy-start | bytes 12292
  420.7 4.1 collective-permute-start.2
  512.6 2.2 copy-start.3
Sparse Core Ops, SparseCore 0:
  83.0 108.5 all-gather.3
  195.1 103.7 all-gather.5
  418.7 53.9 all-reduce.6
  485.8 26.6 all-reduce.8
where the time goes:
time: 524 us; the launch traced here: 522 us
  blocking collectives  169 us (32%)
  matrix products  125 us (24%)
  waiting for transfers between devices  87.1 us (17%)
  local copies, waits for them, and re-layouts  56.4 us (11%)
  other arithmetic  55 us (10%)
  between operations  14.9 us (3%)
  starting transfers between devices  14.6 us (3%)
    all_gather x1, blocking collectives, on_device(): piece_bias = lax.all_gather(key_bias, 'seq', axis=0, tiled=True)  143 us
    dot_general x1, matrix products, on_device(): jnp.einsum('qhd,khd->hqk', query_heads, key_heads, preferred_element_type...  53.1 us
    dot_general x1, matrix products, on_device(): jnp.einsum('hqk,khd->hqd', exponent.astype(jnp.bfloat16), value_heads, pr...  48.7 us
    psum x1, waiting for transfers between devices, on_device(): lax.psum(jnp.dot(mixed, out_weight, preferred_element_type=jnp.float32),...  47.1 us
    reduce_sum x1, other arithmetic, on_device(): total_weight = jnp.sum(exponent, axis=2)  41.2 us
    psum x1, waiting for transfers between devices, on_device(): lax.psum(jnp.dot(hidden, down_weight, preferred_element_type=jnp.float32)...  24.1 us
    unnamed x1, blocking collectives  23.4 us
    all_gather x1, local copies, waits for them, and re-layouts, on_device(): piece_keys = lax.all_gather(key_block, 'seq', axis=0, tiled=True)  21.6 us
  transfers between devices with their start and end apart: 9, of which 5 were waited for; matrix products, arithmetic and copies ran while one was open for 27% of the time, Pallas kernels for 0%

commit v1 on v0

v1 whole, which is shorter than its diff:
```python
import functools
import math

import jax
import jax.numpy as jnp
from jax import lax
from jax.experimental import pallas as pl
from jax.experimental.pallas import tpu as pltpu
from jax.sharding import PartitionSpec as P

HEAD_DIM = 64
LANES = 128
epsilon = 1e-06
empty_bias = -10000.0
LOG2E = math.log2(math.e)
SEQ = "seq"
NT = (((1,), (1,)), ((), ()))
TN = (((0,), (0,)), ((), ()))
NN = (((1,), (0,)), ((), ()))


def layer_norm(values, gain_vector):
    center = values - jnp.mean(values, axis=-1, keepdims=True)
    spread = jnp.mean(center * center, axis=-1, keepdims=True)
    return center * lax.rsqrt(spread + epsilon) * gain_vector


def dot32(a, b, dims=NN):
    return lax.dot_general(a, b, dims, preferred_element_type=jnp.float32)


def swap_cores(values):
    return lax.ppermute(values, "mp", [(0, 1), (1, 0)])


MESH = pl.DeviceIdType.MESH
ORDERS = ((1, 2, 4), (2, 4, 1), (4, 1, 2))
PARTS = ((0, 3), (3, 3), (6, 2))
STEP_OF = {0: 0, 1: 1, 2: 2, 4: 3, 3: 4, 5: 5, 6: 6, 7: 7}


def places():
    me = lax.axis_index("seq")
    return me // 16, me // 4 % 4, me % 4


def near(mask):
    z, y, x = places()
    if mask & 4:
        z = z + 1 - 2 * (z % 2)
    if mask & 2:
        y = y + 1 - 2 * (y % 2)
    if mask & 1:
        x = x + 1 - 2 * (x % 2)
    return z * 16 + y * 4 + x


def far(mask):
    z, y, x = places()
    if mask & 4:
        z = 3 - z
    if mask & 2:
        y = 3 - y
    if mask & 1:
        x = 3 - x
    return z * 16 + y * 4 + x


def cube_index(mask=0):
    z, y, x = places()
    z, y, x = z // 2, y // 2, x // 2
    if mask & 4:
        z = 1 - z
    if mask & 2:
        y = 1 - y
    if mask & 1:
        x = 1 - x
    return z * 4 + y * 2 + x


def layer_kernel(
    rows,
    dropped,
    total_ref,
    balanced_ref,
    bias_ref,
    attn_gain_ref,
    mlp_gain_ref,
    qkv_hbm,
    out_hbm,
    up_hbm,
    down_hbm,
    result_ref,
    qkv_w,
    out_w,
    up_w,
    down_w,
    kv_send,
    q_send,
    kv_buf,
    q_buf,
    k2,
    v2,
    acc,
    peak,
    o_send,
    o_buf,
    part_send,
    part_recv,
    layer_one,
    weight_sem,
    local_sem,
    spread_send,
    spread_recv,
    pass_send,
    pass_recv,
    back_send,
    back_recv,
    core_send,
    core_recv,
):
    core = lax.axis_index("mp")
    heads = 8
    block = rows + 16
    width = balanced_ref.shape[1]

    weight_copies = [
        pltpu.make_async_copy(src, dst, weight_sem.at[i])
        for i, (src, dst) in enumerate(((qkv_hbm, qkv_w), (out_hbm, out_w), (up_hbm, up_w), (down_hbm, down_w)))
    ]
    for copy in weight_copies:
        copy.start()

    barrier = pltpu.get_barrier_semaphore()
    for mask in range(1, 8):
        pl.semaphore_signal(barrier, inc=1, device_id=(far(mask), core), device_id_type=MESH)
    for mask in (1, 2, 4):
        pl.semaphore_signal(barrier, inc=1, device_id=(near(mask), core), device_id_type=MESH)
    pl.semaphore_signal(barrier, inc=1, device_id=(lax.axis_index("seq"), 1 - core), device_id_type=MESH)

    balanced = balanced_ref[:rows].astype(jnp.float32)
    normed = layer_norm(balanced, attn_gain_ref[...]).astype(jnp.bfloat16)
    weight_copies[0].wait()
    pl.semaphore_wait(barrier, 11)

    key = dot32(normed, qkv_w[1]).astype(jnp.bfloat16)
    value = dot32(normed, qkv_w[2]).astype(jnp.bfloat16)
    for j in range(heads):
        columns = slice(j * HEAD_DIM, (j + 1) * HEAD_DIM)
        kv_send[j, :rows, :] = jnp.concatenate([key[:, columns], value[:, columns]], axis=1)
        kv_send[j, rows:, :] = bias_ref[...]

    def spread_kv(mask):
        return pltpu.make_async_remote_copy(
            kv_send.at[cube_index(mask)], kv_buf.at[0, mask], spread_send.at[0, mask], spread_recv.at[0, mask],
            device_id=(far(mask), core), device_id_type=MESH,
        )

    def spread_q(mask):
        return pltpu.make_async_remote_copy(
            q_send.at[cube_index(mask)], q_buf.at[mask], spread_send.at[1, mask], spread_recv.at[1, mask],
            device_id=(far(mask), core), device_id_type=MESH,
        )

    def pass_on(part, near_mask, slot):
        first, size = PARTS[part]
        target = STEP_OF[slot ^ near_mask]
        return pltpu.make_async_remote_copy(
            kv_buf.at[STEP_OF[slot], pl.ds(first, size)], kv_buf.at[target, pl.ds(first, size)],
            pass_send.at[part, target], pass_recv.at[part, target],
            device_id=(near(near_mask), core), device_id_type=MESH,
        )

    for mask in range(1, 8):
        spread_kv(mask).start()
    own_kv = pltpu.make_async_copy(kv_send.at[cube_index()], kv_buf.at[0, 0], local_sem.at[0])
    own_kv.start()
    query = (dot32(normed, qkv_w[0]) * (HEAD_DIM ** (-0.5) * LOG2E)).astype(jnp.bfloat16)
    ones = (lax.broadcasted_iota(jnp.int32, (rows, HEAD_DIM), 1) < 2).astype(jnp.bfloat16)
    for j in range(heads):
        q_send[j] = jnp.concatenate([query[:, j * HEAD_DIM : (j + 1) * HEAD_DIM], ones], axis=1)
    for mask in range(1, 8):
        spread_q(mask).start()
    own_q = pltpu.make_async_copy(q_send.at[cube_index()], q_buf.at[0], local_sem.at[1])
    own_q.start()
    own_kv.wait()
    own_q.wait()
    for mask in range(1, 8):
        spread_kv(mask).wait_recv()
    for order in range(3):
        for part in range(3):
            pass_on(part, ORDERS[part][order], 0).start()
    for mask in range(1, 8):
        spread_q(mask).wait_recv()

    queries = heads * rows
    cut = queries // 2 // 256 * 256
    acc[...] = jnp.zeros_like(acc)
    empty = -9984.0 * LOG2E
    peak[...] = jnp.full(peak.shape, empty if dropped else -3e38, jnp.float32)
    lane = lax.broadcasted_iota(jnp.int32, (rows, LANES), 1)
    value_tail = (lane == HEAD_DIM).astype(jnp.bfloat16)
    if dropped:
        acc[HEAD_DIM : HEAD_DIM + 1, :] = jnp.full((1, queries), float(dropped), jnp.float32)
    pick_row = lax.broadcasted_iota(jnp.int32, (16, LANES), 0)
    pick_lane = lax.broadcasted_iota(jnp.int32, (16, LANES), 1)
    picks = [
        (((pick_row == i) & (pick_lane == HEAD_DIM)) | ((pick_row == i + 2) & (pick_lane == HEAD_DIM + 1))).astype(jnp.bfloat16)
        for i in range(2)
    ]

    def step(i, carry):
        for slot, at in STEP_OF.items():
            if slot == 0:
                continue

            @pl.when(i == at)
            def _(slot=slot):
                for part in range(3):
                    d1, d2, d3 = ORDERS[part]
                    came_by = d3 if slot & d3 else d2 if slot & d2 else d1
                    pass_on(part, came_by, slot ^ came_by).wait_recv()
                    if came_by == d1:
                        pass_on(part, d2, slot).start()
                    if came_by != d3:
                        pass_on(part, d3, slot).start()

        def unpack(a, carry):
            here = pl.ds(pl.multiple_of(a * rows, 16), rows)
            kv = kv_buf[i, a, :rows, :]
            tile = kv_buf[i, a, rows:, :]
            bias = jnp.concatenate(
                [dot32(tile, picks[0], TN), dot32(tile, picks[1], TN)], axis=0
            )[:rows].astype(jnp.bfloat16)
            k2[here, :] = jnp.where(lane < HEAD_DIM, kv, bias)
            v2[here, :] = jnp.concatenate([kv[:, HEAD_DIM:], value_tail[:, HEAD_DIM:]], axis=1)
            return carry

        lax.fori_loop(0, heads, unpack, 0)
        for begin, end in ((0, cut), (cut, queries)):
            first_a = begin
            q = q_buf[...].reshape(queries, LANES)[begin:end]
            s = dot32(k2[...], q, NT)
            old = peak[:, begin:end]
            new = jnp.maximum(old, jnp.max(s, axis=0, keepdims=True))
            p = jnp.exp2(s - new).astype(jnp.bfloat16)
            peak[:, begin:end] = new
            acc[:, begin:end] = acc[:, begin:end] * jnp.exp2(old - new) + dot32(v2[...], p, TN)
        return carry

    lax.fori_loop(0, 8, step, 0)

    def back(mask):
        return pltpu.make_async_remote_copy(
            o_send.at[mask], o_buf.at[cube_index()], back_send.at[mask], back_recv.at[mask],
            device_id=(far(mask), core), device_id_type=MESH,
        )

    def back_in(mask):
        return pltpu.make_async_remote_copy(
            o_send.at[mask], o_buf.at[cube_index(mask)], back_send.at[mask], back_recv.at[mask],
            device_id=(far(mask), core), device_id_type=MESH,
        )

    scaled = acc[...] / acc[HEAD_DIM : HEAD_DIM + 1, :]
    o_send[...] = scaled.T.astype(jnp.bfloat16).reshape(heads, rows, LANES)
    for mask in range(1, 8):
        back(mask).start()
    own_o = pltpu.make_async_copy(o_send.at[0], o_buf.at[cube_index()], local_sem.at[2])
    own_o.start()
    weight_copies[1].wait()
    own_o.wait()
    for mask in range(1, 8):
        back_in(mask).wait_recv()

    def swap(which, size):
        return pltpu.make_async_remote_copy(
            part_send.at[which], part_recv.at[which], core_send.at[which], core_recv.at[which],
            device_id=(lax.axis_index("seq"), 1 - core), device_id_type=MESH,
        )

    mixed = jnp.concatenate([o_buf[j, :, :HEAD_DIM] for j in range(heads)], axis=1)
    part_send[0] = dot32(mixed, out_w[...]).astype(jnp.bfloat16)
    swap(0, rows).start()
    swap(0, rows).wait_recv()
    attention = part_send[0].astype(jnp.float32) + part_recv[0].astype(jnp.float32)
    layer_one[...] = (balanced_ref[:rows].astype(jnp.float32) + attention).astype(jnp.bfloat16)
    normed_mlp = layer_norm(layer_one[...].astype(jnp.float32), mlp_gain_ref[...]).astype(jnp.bfloat16)
    weight_copies[2].wait()
    weight_copies[3].wait()
    hidden = dot32(normed_mlp, up_w[...])
    hidden = (0.5 * hidden * (1.0 + lax.erf(hidden * math.sqrt(0.5)))).astype(jnp.bfloat16)
    part_send[1] = dot32(hidden, down_w[...]).astype(jnp.bfloat16)
    swap(1, rows).start()
    swap(1, rows).wait_recv()
    mlp = part_send[1].astype(jnp.float32) + part_recv[1].astype(jnp.float32)
    result = layer_one[...].astype(jnp.float32) + mlp
    slot = lax.broadcasted_iota(jnp.int32, (rows, width), 0) * 64 + lax.axis_index("seq")
    result_ref[:rows, :] = jnp.where(slot < total_ref[0], result, 0.0).astype(jnp.bfloat16)
    if rows < result_ref.shape[0]:
        result_ref[rows:, :] = jnp.zeros((result_ref.shape[0] - rows, width), jnp.bfloat16)

    for mask in range(1, 8):
        spread_kv(mask).wait_send()
        spread_q(mask).wait_send()
        back(mask).wait_send()
    for part in range(3):
        d1, d2, d3 = ORDERS[part]
        for near_mask, slot in ((d1, 0), (d2, 0), (d3, 0), (d2, d1), (d3, d1), (d3, d2), (d3, d1 | d2)):
            pass_on(part, near_mask, slot).wait_send()
    swap(0, rows).wait_send()
    swap(1, rows).wait_send()


def layer(rows, which, total, balanced, bias_tile, attn_gain, mlp_gain, qkv_weight, out_weight, up_weight, down_weight):
    total_rows, width = balanced.shape
    heads = 8
    hidden = up_weight.shape[1]
    queries = heads * rows
    bf16 = jnp.bfloat16
    vmem = pl.BlockSpec(memory_space=pltpu.VMEM)
    anywhere = pl.BlockSpec(memory_space=pl.ANY)
    dma = pltpu.SemaphoreType.DMA
    return pl.pallas_call(
        functools.partial(layer_kernel, rows, 64 * (total_rows - rows)),
        in_specs=[pl.BlockSpec(memory_space=pltpu.SMEM), vmem, vmem, vmem, vmem] + [anywhere] * 4,
        out_specs=vmem,
        out_shape=jax.ShapeDtypeStruct((total_rows, width), bf16),
        scratch_shapes=[
            pltpu.VMEM(qkv_weight.shape, bf16),
            pltpu.VMEM(out_weight.shape, bf16),
            pltpu.VMEM(up_weight.shape, bf16),
            pltpu.VMEM(down_weight.shape, bf16),
            pltpu.VMEM((heads, rows + 16, LANES), bf16),
            pltpu.VMEM((heads, rows, LANES), bf16),
            pltpu.VMEM((8, heads, rows + 16, LANES), bf16),
            pltpu.VMEM((heads, rows, LANES), bf16),
            pltpu.VMEM((queries, LANES), bf16),
            pltpu.VMEM((queries, LANES), bf16),
            pltpu.VMEM((LANES, queries), jnp.float32),
            pltpu.VMEM((1, queries), jnp.float32),
            pltpu.VMEM((heads, rows, LANES), bf16),
            pltpu.VMEM((heads, rows, LANES), bf16),
            pltpu.VMEM((2, rows, width), bf16),
            pltpu.VMEM((2, rows, width), bf16),
            pltpu.VMEM((rows, width), bf16),
            dma((4,)),
            dma((3,)),
            dma((2, 8)),
            dma((2, 8)),
            dma((3, 8)),
            dma((3, 8)),
            dma((8,)),
            dma((8,)),
            dma((2,)),
            dma((2,)),
        ],
        compiler_params=pltpu.CompilerParams(
            vmem_limit_bytes=60 * 2**20, collective_id=which, has_side_effects=True
        ),
        cost_estimate=pl.CostEstimate(
            flops=queries * queries * 8 * 256, bytes_accessed=16 * 2**20, transcendentals=queries * queries * 8
        ),
    )(total, balanced, bias_tile, attn_gain, mlp_gain, qkv_weight, out_weight, up_weight, down_weight)


def on_device(
    tokens,
    token_sizes,
    merge_source,
    merge_target,
    merge_count,
    attn_gain,
    qkv_weight,
    out_weight,
    mlp_gain,
    up_weight,
    down_weight,
):
    shards = 64
    me = lax.axis_index(SEQ)
    rows, width = tokens.shape
    half = rows // 2
    slots = rows // shards
    ids = jnp.arange(half, dtype=jnp.int32)
    row_ids = jnp.arange(rows, dtype=jnp.int32)
    shard_ids = jnp.arange(shards, dtype=jnp.int32)
    ahead = [(i, (i + 1) % shards) for i in range(shards)]
    behind = [(i, (i - 1) % shards) for i in range(shards)]

    counts = rows - lax.all_gather(merge_count, SEQ, axis=0, tiled=True)
    active = ids < merge_count[0]
    hit = (merge_source[0][:, None] == ids[None, :]) & active[:, None]
    removed = jnp.any(hit, axis=0)
    goal = jnp.sum(jnp.where(hit, merge_target[0][:, None], 0), axis=0)
    weights = jnp.where(
        (goal[None, :] == ids[:, None]) & removed[None, :], token_sizes[half:][None, :], 0
    ).astype(jnp.bfloat16)
    merging = lax.ppermute(jnp.concatenate([tokens[half:], weights], axis=1), SEQ, ahead)
    weights = merging[:, width:]
    added_rows = dot32(weights, merging[:, :width])
    added_size = jnp.sum(weights.astype(jnp.float32), axis=1)
    base_size = token_sizes[:half].astype(jnp.float32)
    merged = (base_size[:, None] * tokens[:half].astype(jnp.float32) + added_rows) / (
        base_size + added_size
    )[:, None]
    new_rows = jnp.concatenate([merged.astype(jnp.bfloat16), tokens[half:]], axis=0)
    new_size = jnp.concatenate([base_size + added_size, token_sizes[half:].astype(jnp.float32)])
    bias_rows = jnp.log(new_size).astype(jnp.bfloat16)
    bias_lanes = jnp.where(jnp.arange(LANES)[None, :] == 0, bias_rows[:, None], 0).astype(jnp.bfloat16)
    payload = jnp.concatenate([new_rows, bias_lanes], axis=1)

    survive = jnp.concatenate([jnp.ones((half,), bool), jnp.logical_not(removed)])
    local_rank = jnp.sum((row_ids[:, None] > row_ids[None, :]) & survive[None, :], axis=1, dtype=jnp.int32)
    before = jnp.sum(jnp.where(shard_ids[:, None] > shard_ids[None, :], counts[None, :], 0), axis=1)
    my_start = jnp.sum(jnp.where(shard_ids < me, counts, 0))
    grand_total = jnp.sum(counts)
    flat_slot = (my_start + local_rank) % shards * slots + local_rank // shards
    put = ((flat_slot[None, :] == row_ids[:, None]) & survive[None, :]).astype(jnp.bfloat16)
    outgoing = dot32(put, payload).astype(jnp.bfloat16).reshape(shards, slots, width + LANES)
    arrived = lax.all_to_all(outgoing, SEQ, split_axis=0, concat_axis=0, tiled=True)
    wanted = row_ids * shards + me
    filled = wanted < grand_total
    sender = jnp.sum((before[None, :] <= wanted[:, None]).astype(jnp.int32), axis=1) - 1
    sender_start = jnp.sum(jnp.where(sender[:, None] == shard_ids[None, :], before[None, :], 0), axis=1)
    fetch = sender * slots + (wanted - sender_start) // shards
    take = ((fetch[:, None] == row_ids[None, :]) & filled[:, None]).astype(jnp.bfloat16)
    balanced = dot32(take, arrived.reshape(rows, width + LANES)).astype(jnp.bfloat16)
    key_bias = jnp.where(filled, balanced[:, width], jnp.bfloat16(empty_bias))
    balanced = balanced[:, :width]

    bias = key_bias.astype(jnp.float32) * LOG2E
    high = bias.astype(jnp.bfloat16)
    low = (bias - high.astype(jnp.float32)).astype(jnp.bfloat16)
    bias_tile = jnp.concatenate(
        [high.reshape(2, LANES), low.reshape(2, LANES), jnp.zeros((12, LANES), jnp.bfloat16)], axis=0
    )
    sizes = (192, 208, rows)
    needed = (grand_total + shards - 1) // shards
    index = sum((needed > size).astype(jnp.int32) for size in sizes[:-1])
    merged_out = lax.switch(
        index,
        [functools.partial(layer, size, at + 1) for at, size in enumerate(sizes)],
        grand_total[None], balanced, bias_tile, attn_gain[None, :], mlp_gain[None, :],
        qkv_weight, out_weight, up_weight, down_weight,
    )

    normed = layer_norm(tokens.astype(jnp.float32), attn_gain).astype(jnp.bfloat16)
    metric = dot32(normed, qkv_weight[1]).astype(jnp.bfloat16)
    partner = lax.ppermute(metric[:half], SEQ, behind)
    own_keys = metric[half:]
    products = dot32(own_keys, partner, NT)
    own_square = jnp.sum(jnp.square(own_keys.astype(jnp.float32)), axis=1)
    partner_square = jnp.sum(jnp.square(partner.astype(jnp.float32)), axis=1)
    sums = jnp.concatenate(
        [products, jnp.broadcast_to(own_square[:, None], (half, LANES)), jnp.broadcast_to(partner_square[:, None], (half, LANES))], axis=1
    )
    sums = sums + swap_cores(sums)
    cosine = (
        sums[:, :LANES]
        * lax.rsqrt(sums[:, LANES] + epsilon)[:, None]
        * lax.rsqrt(sums[:, 2 * LANES] + epsilon)[None, :]
    )
    best_score = jnp.max(cosine, axis=1)
    return (merged_out, best_score)


def solution(mesh):
    placed = (
        P(SEQ, None),
        P(SEQ),
        P(SEQ, None),
        P(SEQ, None),
        P(SEQ),
        P(),
        P(None, None, "mp"),
        P("mp", None),
        P(),
        P(None, "mp"),
        P("mp", None),
    )
    return jax.shard_map(
        on_device, mesh=mesh, in_specs=placed, out_specs=(P(SEQ, None), P(SEQ)), check_vma=False
    )
```

time: 524 us -> 148 us (0.28)
  blocking collectives: 169 us -> 13.5 us
  matrix products: 125 us -> 2.89 us
  Pallas kernels: 0 us -> 81.5 us
  waiting for transfers between devices: 87.1 us -> 11.4 us
  local copies, waits for them, and re-layouts: 56.4 us -> 4.5 us
  other arithmetic: 55 us -> 7.07 us
  between operations: 14.9 us -> 2.31 us
  starting transfers between devices: 14.6 us -> 23 us
    all_gather x1 -> x0, blocking collectives: 143 us -> none  [on_device(): piece_bias = lax.all_gather(key_bias, 'seq', axis=0, tiled=True)]
    dot_general x10 -> x5, matrix products: 125 us -> 2.89 us  [dot32(): return lax.dot_general(a, b, dims, preferred_element_type=jnp.float32)]
    pallas_call x0 -> x1, Pallas kernels: none -> 81.5 us  [layer(): pl.pallas_call(functools.partial(layer_kernel, rows, 64 * (total_rows - r...]
    psum x2 -> x0, waiting for transfers between devices: 71.2 us -> none  [the longest x1 47.1 us: on_device(): lax.psum(jnp.dot(mixed, out_weight, preferred_element_type=jnp.float32),...]
    all_gather x2 -> x0, local copies, waits for them, and re-layouts: 42.8 us -> none  [the longest x1 21.6 us: on_device(): piece_keys = lax.all_gather(key_block, 'seq', axis=0, tiled=True)]
    reduce_sum x3 -> x4, other arithmetic: 42.5 us -> 1.66 us  [the longest x1 0.8 us: on_device(): goal = jnp.sum(jnp.where(hit, merge_target[0][:, None], 0), axis=0)]
    ppermute x3, starting transfers between devices: 4.4 us -> 15.5 us  [the longest x1 7.27 us: on_device(): partner = lax.ppermute(metric[:half], SEQ, behind)]
    unnamed x1, blocking collectives: 23.4 us -> 13.5 us
  transfers between devices with their start and end apart: 9 -> 4, of which waited for: 5 -> 1; matrix products, arithmetic and copies ran while one was open for 27% -> 6% of each run, Pallas kernels for 0% -> 0%
where the time goes in v1:
time: 148 us; the launch traced here: 147 us
  Pallas kernels  81.5 us (55%)
  starting transfers between devices  23 us (16%)
  blocking collectives  13.5 us (9%)
  waiting for transfers between devices  11.4 us (8%)
  other arithmetic  7.07 us (5%)
  local copies, waits for them, and re-layouts  4.5 us (3%)
  matrix products  2.89 us (2%)
  between operations  2.31 us (2%)
    pallas_call x1, Pallas kernels, layer(): pl.pallas_call(functools.partial(layer_kernel, rows, 64 * (total_rows - r...  81.5 us
    unnamed x1, blocking collectives  13.5 us
    all_to_all x1, waiting for transfers between devices, on_device(): lax.all_to_all(outgoing, SEQ, split_axis=0, concat_axis=0, tiled=True)  11.4 us
    all_to_all x1, starting transfers between devices, on_device(): lax.all_to_all(outgoing, SEQ, split_axis=0, concat_axis=0, tiled=True)  7.48 us
    ppermute x1, starting transfers between devices, on_device(): partner = lax.ppermute(metric[:half], SEQ, behind)  7.27 us
    ppermute x1, starting transfers between devices, swap_cores(): return lax.ppermute(values, 'mp', [(0, 1), (1, 0)])  6.16 us
  transfers between devices with their start and end apart: 4, of which 1 were waited for; matrix products, arithmetic and copies ran while one was open for 6% of the time, Pallas kernels for 0%

profile of v1, /device:TPU:1, one launch (start us, length us, event | category | flops | bytes accessed | tf_op | source)
XLA Modules:
  0.0 147.1 jit_solution(8034135537824166507)
XLA Ops:
  1.4 0.8 fusion.33
  2.1 0.8 select_reduce_fusion
  2.9 0.8 slice_convert_fusion
  3.7 1.0 slice.46
  4.7 2.1 %collective-permute-start = (bf16[128,1152]{1,0:T(8,128)(2,1)S(1)}, bf16[128,1152]{1,0:T(8,128)(2,1)S(1)}, u32[]{:S(2)}, u32[]{:S(2)}) collective-permute-start(bf16[128,1152]{1,0:T(8,128)(2,1)S(1)} %pad_maximum_fusion), channel_id=1, source_target_pairs={{0,2},{2,4},{4,6},{6,8},{8,10},{10,12},{12,14},{14,16},{16,18},{18... | collective-permute-start | bytes 884744 | tf_op jit(solution)/shard_map/ppermute | solution.py:399
  7.3 1.7 %convolution_convert_fusion.2 = bf16[256,512]{1,0:T(8,128)(2,1)S(1)} fusion(bf16[3,1024,512]{2,1,0:T(8,128)(2,1)} %param.20, bf16[256,1024]{1,0:T(8,128)(2,1)S(1)} %copy-done, f32[1024]{0:T(1024)S(1)} %copy-done.3, f32[256]{0:T(256)S(1)} %add_rsqrt_fusion, f32[256]{0:T(256)S(1)} %broadcast_multiply_fusion), kind=kOutput, calls=%fused_computation.9 | convolution fusion | flops 269877248 | bytes 1841152 | tf_op jit(solution)/shard_map/dot_general | solution.py:29
  9.1 7.3 %collective-permute-start.1 = (bf16[128,512]{1,0:T(8,128)(2,1)S(1)}, bf16[128,512]{1,0:T(8,128)(2,1)S(1)}, u32[]{:S(2)}, u32[]{:S(2)}) collective-permute-start(bf16[128,512]{1,0:T(8,128)(2,1)S(1)} %slice.63), channel_id=1, source_target_pairs={{0,126},{2,0},{4,2},{6,4},{8,6},{10,8},{12,10},{14,12},{16,14},{18... | collective-permute-start | bytes 393224 | tf_op jit(solution)/shard_map/ppermute | solution.py:450
  16.4 0.6 dynamic-slice
  17.0 0.8 dynamic-update-slice
  17.7 13.5 %all-reduce.1 = s32[64]{0:T(128)S(1)} all-reduce(s32[64]{0:T(128)S(1)} %dynamic-update-slice), channel_id=1, replica_groups=mesh['seq'=64,'mp'=2] {'seq'}, use_global_device_ids=true, to_apply=%add.1 | all-reduce | flops 64 | bytes 512
  31.2 0.6 fusion.43
  32.3 0.7 fusion.38
  33.4 6.2 %collective-permute-start.2 = (f32[128,384]{0,1:T(8,128)S(1)}, f32[128,384]{0,1:T(8,128)S(1)}, u32[]{:S(2)}, u32[]{:S(2)}) collective-permute-start(f32[128,384]{0,1:T(8,128)S(1)} %pad_maximum_fusion.1), channel_id=1, source_target_pairs={{0,1},{1,0},{2,3},{3,2},{4,5},{5,4},{6,7},{7,6},{8,9},{9,8},{10,11... | collective-permute-start | bytes 589832 | tf_op jit(solution)/shard_map/ppermute | solution.py:33
  40.1 0.4 convolution_convert_fusion.1
  40.4 0.9 reshape.141
  41.4 7.5 %all-to-all-start = ((bf16[64,4,1152]{2,1,0:T(4,128)(2,1)}), bf16[64,4,1152]{2,1,0:T(4,128)(2,1)S(1)}, u32[]{:S(2)}, u32[]{:S(2)}) async-start(bf16[64,4,1152]{2,1,0:T(4,128)(2,1)} %reshape.141), calls=%async_computation | async-start | bytes 1179648 | tf_op jit(solution)/shard_map/all_to_all | solution.py:421
  48.9 0.7 broadcast_compare_fusion
  50.3 0.6 fusion.31
  51.0 11.4 %all-to-all-done = bf16[64,4,1152]{2,1,0:T(4,128)(2,1)S(1)} async-done(((bf16[64,4,1152]{2,1,0:T(4,128)(2,1)}), bf16[64,4,1152]{2,1,0:T(4,128)(2,1)S(1)}, u32[]{:S(2)}, u32[]{:S(2)}) %all-to-all-start) | async-done | bytes 589856 | tf_op jit(solution)/shard_map/all_to_all | solution.py:421
  62.5 0.4 convolution_convert_fusion
  63.1 0.7 fusion.41
  63.9 82.5 %conditional.1 = (bf16[256,1024]{1,0:T(8,128)(2,1)S(1)}) conditional(s32[]{:T(128)} %clamp.3, (s32[1]{0:T(128)}, bf16[256,1024]{1,0:T(8,128)(2,1)S(1)}, bf16[16,128]{1,0:T(8,128)(2,1)S(1)}, f32[1,1024]{1,0:T(1,128)S(1)}, f32[1,1024]{1,0:T(1,128)S(1)}, /*index=5*/bf16[3,1024,512]{2,1,0:T(8,128)(2,1)}, ...), branch_computations={%region_9.10_spmd, %region_10.11_spmd, %region_11.12_spmd} | conditional | flops 8589934592 | bytes 16777224 | solution.py:441
  64.3 81.5 %branch_1_fun.1 = bf16[256,1024]{1,0:T(8,128)(2,1)S(1)} custom-call(s32[1]{0:T(128)} %get-tuple-element.67.total_ref, bf16[256,1024]{1,0:T(8,128)(2,1)S(1)} %get-tuple-element.68.balanced_ref, bf16[16,128]{1,0:T(8,128)(2,1)S(1)} %get-tuple-element.69.bias_ref, f32[1,1024]{1,0:T(1,128)S(1)} %get-tuple-element.70.attn_gain_ref, ...), custom_call_target="tpu_custom_call" | custom-call | flops 5670699008 | bytes 16777216 | tf_op jit(solution)/shard_map/cond/branch_1_fun/pallas_call | solution.py:324
  146.3 0.8 copy.19
  (53 shorter events, 2.4 us)
Async XLA Ops:
  0.6 6.2 %copy-start = (bf16[256,1024]{1,0:T(8,128)(2,1)S(1)}, bf16[256,1024]{1,0:T(8,128)(2,1)}, u32[]{:S(2)}) copy-start(bf16[256,1024]{1,0:T(8,128)(2,1)} %param.14) | copy-start | bytes 1572868
  0.6 6.7 %copy-start.3 = (f32[1024]{0:T(1024)S(1)}, f32[1024]{0:T(1024)}, u32[]{:S(2)}) copy-start(f32[1024]{0:T(1024)} %param.19) | copy-start | bytes 12292
  4.7 34.9 %collective-permute-start = (bf16[128,1152]{1,0:T(8,128)(2,1)S(1)}, bf16[128,1152]{1,0:T(8,128)(2,1)S(1)}, u32[]{:S(2)}, u32[]{:S(2)}) collective-permute-start(bf16[128,1152]{1,0:T(8,128)(2,1)S(1)} %pad_maximum_fusion), channel_id=1, source_target_pairs={{0,2},{2,4},{4,6},{6,8},{8,10},{10,12},{12,14},{14,16},{16,18},{18... | collective-permute-start | bytes 884744 | tf_op jit(solution)/shard_map/ppermute | solution.py:399
  7.3 9.1 %copy-start.5 = (u32[128]{0:T(128)S(1)}, u32[128]{0:T(128)}, u32[]{:S(2)}) copy-start(u32[128]{0:T(128)} %constant.100) | copy-start | bytes 1540
  9.1 30.6 %copy-start.1 = (s32[256]{0:T(256)S(1)}, s32[256]{0:T(256)}, u32[]{:S(2)}) copy-start(s32[256]{0:T(256)} %param.15) | copy-start | bytes 3076
  9.1 24.0 %collective-permute-start.1 = (bf16[128,512]{1,0:T(8,128)(2,1)S(1)}, bf16[128,512]{1,0:T(8,128)(2,1)S(1)}, u32[]{:S(2)}, u32[]{:S(2)}) collective-permute-start(bf16[128,512]{1,0:T(8,128)(2,1)S(1)} %slice.63), channel_id=1, source_target_pairs={{0,126},{2,0},{4,2},{6,4},{8,6},{10,8},{12,10},{14,12},{16,14},{18... | collective-permute-start | bytes 393224 | tf_op jit(solution)/shard_map/ppermute | solution.py:450
  33.4 16.9 %collective-permute-start.2 = (f32[128,384]{0,1:T(8,128)S(1)}, f32[128,384]{0,1:T(8,128)S(1)}, u32[]{:S(2)}, u32[]{:S(2)}) collective-permute-start(f32[128,384]{0,1:T(8,128)S(1)} %pad_maximum_fusion.1), channel_id=1, source_target_pairs={{0,1},{1,0},{2,3},{3,2},{4,5},{5,4},{6,7},{7,6},{8,9},{9,8},{10,11... | collective-permute-start | bytes 589832 | tf_op jit(solution)/shard_map/ppermute | solution.py:33
  41.4 21.0 %all-to-all-start = ((bf16[64,4,1152]{2,1,0:T(4,128)(2,1)}), bf16[64,4,1152]{2,1,0:T(4,128)(2,1)S(1)}, u32[]{:S(2)}, u32[]{:S(2)}) async-start(bf16[64,4,1152]{2,1,0:T(4,128)(2,1)} %reshape.141), calls=%async_computation | async-start | bytes 1179648 | tf_op jit(solution)/shard_map/all_to_all | solution.py:421
  62.5 1.3 copy-start.2
  62.5 1.3 copy-start.4

commit v2 on v1

--- a/solution.py
+++ b/solution.py
@@ -11,9 +11,7 @@
 HEAD_DIM = 64
 LANES = 128
 epsilon = 1e-06
-empty_bias = -10000.0
 LOG2E = math.log2(math.e)
-SEQ = "seq"
 NT = (((1,), (1,)), ((), ()))
 TN = (((0,), (0,)), ((), ()))
 NN = (((1,), (0,)), ((), ()))
@@ -27,10 +25,6 @@
 
 def dot32(a, b, dims=NN):
     return lax.dot_general(a, b, dims, preferred_element_type=jnp.float32)
-
-
-def swap_cores(values):
-    return lax.ppermute(values, "mp", [(0, 1), (1, 0)])
 
 
 MESH = pl.DeviceIdType.MESH
@@ -364,6 +358,311 @@
     )(total, balanced, bias_tile, attn_gain, mlp_gain, qkv_weight, out_weight, up_weight, down_weight)
 
 
+def near_index(mask=0):
+    z, y, x = places()
+    bits = [(c // 2 + c % 2) % 2 for c in (z, y, x)]
+    bits = [1 - b if mask & m else b for b, m in zip(bits, (4, 2, 1))]
+    return bits[0] * 4 + bits[1] * 2 + bits[2]
+
+
+def cube_and_near(shard):
+    parts = (shard >> 4, (shard >> 2) & 3, shard & 3)
+    cube = sum((c >> 1) * m for c, m in zip(parts, (4, 2, 1)))
+    near = sum(((c >> 1) ^ (c & 1)) * m for c, m in zip(parts, (4, 2, 1)))
+    return cube, near
+
+
+def iota(shape, dim):
+    return lax.broadcasted_iota(jnp.int32, shape, dim)
+
+
+def to_column(row):
+    n = row.shape[1]
+    return jnp.sum(jnp.where(iota((n, n), 0) == iota((n, n), 1), row, 0), axis=1, keepdims=True)
+
+
+def to_row(column):
+    n = column.shape[0]
+    return jnp.sum(jnp.where(iota((n, n), 0) == iota((n, n), 1), column, 0), axis=0, keepdims=True)
+
+
+def deal_kernel(
+    tokens_ref,
+    sizes_ref,
+    source_ref,
+    target_ref,
+    count_ref,
+    gain_ref,
+    key_w,
+    balanced_ref,
+    bias_ref,
+    total_ref,
+    best_ref,
+    shift_send,
+    shift_recv,
+    count_send,
+    count_recv,
+    metric_send,
+    metric_recv,
+    score_send,
+    score_recv,
+    far_out,
+    far_in,
+    near_out,
+    near_in,
+    half_send,
+    half_recv,
+    shift_sem,
+    count_send_sem,
+    count_recv_sem,
+    metric_sem,
+    score_sem,
+    far_send_sem,
+    far_recv_sem,
+    near_send_sem,
+    near_recv_sem,
+    half_sem,
+    local_sem,
+):
+    me = lax.axis_index("seq")
+    core = lax.axis_index("mp")
+    shards = 64
+    rows, width = tokens_ref.shape
+    half = rows // 2
+    part = width // 2
+    slots = rows // shards
+    ahead, behind = (me + 1) % shards, (me + shards - 1) % shards
+    own_columns = pl.ds(pl.multiple_of(core * part, part), part)
+    f32, bf16 = jnp.float32, jnp.bfloat16
+
+    barrier = pltpu.get_barrier_semaphore()
+    for mask in range(1, 8):
+        pl.semaphore_signal(barrier, inc=1, device_id=(far(mask), core), device_id_type=MESH)
+        pl.semaphore_signal(barrier, inc=1, device_id=(near(mask), core), device_id_type=MESH)
+    for other in (ahead, behind):
+        pl.semaphore_signal(barrier, inc=1, device_id=(other, core), device_id_type=MESH)
+    pl.semaphore_signal(barrier, inc=1, device_id=(me, 1 - core), device_id_type=MESH)
+
+    def remote(src, dst, send_sem, recv_sem, seq, mp):
+        return pltpu.make_async_remote_copy(
+            src, dst, send_sem, recv_sem, device_id=(seq, mp), device_id_type=MESH
+        )
+
+    shift = remote(shift_send, shift_recv, shift_sem.at[0], shift_sem.at[1], ahead, core)
+    metric_copy = remote(metric_send, metric_recv, metric_sem.at[0], metric_sem.at[1], behind, core)
+    score_copy = remote(score_send, score_recv, score_sem.at[0], score_sem.at[1], me, 1 - core)
+    half_copy = remote(half_send, half_recv, half_sem.at[0], half_sem.at[1], me, 1 - core)
+
+    def counts_to(stage, mask):
+        return remote(
+            count_send.at[stage], count_recv.at[stage, mask], count_send_sem.at[stage, mask],
+            count_recv_sem.at[stage, mask], (far, near)[stage](mask), core,
+        )
+
+    def far_copy(mask, landed=False):
+        return remote(
+            far_out.at[cube_index(mask)], far_in.at[cube_index(mask) if landed else cube_index()],
+            far_send_sem.at[mask], far_recv_sem.at[mask], far(mask), core,
+        )
+
+    def near_copy(mask, landed=False):
+        return remote(
+            near_out.at[near_index(mask)], near_in.at[near_index(mask) if landed else near_index()],
+            near_send_sem.at[mask], near_recv_sem.at[mask], near(mask), core,
+        )
+
+    count = count_ref[0]
+    active = iota((1, half), 1) < count
+    hit = (source_ref[...] == iota((half, half), 0)) & active
+    removed = jnp.max(jnp.where(hit, 1, 0), axis=1, keepdims=True)
+    goal = jnp.sum(jnp.where(hit, target_ref[...], 0), axis=1, keepdims=True)
+    late_size = to_column(sizes_ref[:, half:])
+    weights = jnp.where((goal == iota((half, half), 1)) & (removed > 0), late_size, 0)
+    shift_send[:, :part] = tokens_ref[half:, own_columns]
+    shift_send[:, part:] = weights.astype(f32).astype(bf16)
+    lanes = iota((8, LANES), 1)
+    count_send[0] = jnp.where(lanes == me, rows - count, 0).astype(f32)
+
+    pl.semaphore_wait(barrier, 17)
+    shift.start()
+    for mask in range(1, 8):
+        counts_to(0, mask).start()
+
+    normed = layer_norm(tokens_ref[...].astype(f32), gain_ref[...]).astype(bf16)
+    metric = dot32(normed, key_w[...]).astype(bf16)
+    metric_send[...] = metric[:half]
+    metric_copy.start()
+
+    for mask in range(1, 8):
+        counts_to(0, mask).wait_recv()
+    total = count_send[0]
+    for mask in range(1, 8):
+        total = total + count_recv[0, mask]
+    count_send[1] = total
+    for mask in range(1, 8):
+        counts_to(1, mask).start()
+
+    survive = jnp.concatenate([jnp.ones((1, half), f32), 1.0 - to_row(removed.astype(f32))], axis=1)
+    upper = (iota((rows, rows), 0) < iota((rows, rows), 1)).astype(bf16)
+    local_rank = dot32(jnp.broadcast_to(survive, (16, rows)).astype(bf16), upper)[:1].astype(jnp.int32)
+    early_size = to_column(sizes_ref[:, :half]).astype(f32)
+
+    shift.wait_recv()
+    came = shift_recv[:, part:]
+    added_size = dot32(came, jnp.ones((half, LANES), bf16), TN)[:, :1]
+    added_rows = dot32(came, shift_recv[:, :part], TN)
+    new_size = early_size + added_size
+    merged = (early_size * tokens_ref[:half, own_columns].astype(f32) + added_rows) / new_size
+    biases = jnp.log(jnp.concatenate([new_size, late_size.astype(f32)], axis=0))
+    payload = jnp.concatenate(
+        [
+            jnp.concatenate([merged.astype(bf16), tokens_ref[half:, own_columns]], axis=0),
+            jnp.where(iota((rows, LANES), 1) == 0, biases, 0.0).astype(bf16),
+        ],
+        axis=1,
+    )
+
+    for mask in range(1, 8):
+        counts_to(1, mask).wait_recv()
+    total = count_send[1]
+    for mask in range(1, 8):
+        total = total + count_recv[1, mask]
+    counts = total[:1]
+    before = dot32(
+        total.astype(bf16), (iota((LANES, LANES), 0) < iota((LANES, LANES), 1)).astype(bf16)
+    )[:1].astype(jnp.int32)
+    shard_lane = iota((1, LANES), 1)
+    start = jnp.sum(jnp.where(shard_lane == me, before, 0), axis=1, keepdims=True)
+    everyone = jnp.sum(counts, axis=1, keepdims=True).astype(jnp.int32)
+    owner_cube, owner_near = cube_and_near((start + local_rank) & (shards - 1))
+    spot = owner_cube * 32 + owner_near * slots + (local_rank >> 6)
+    spot = jnp.where(survive > 0, spot, rows)
+    put = (spot == iota((rows, rows), 0)).astype(bf16)
+    far_out[...] = dot32(put, payload).astype(bf16).reshape(far_out.shape)
+    for mask in range(1, 8):
+        far_copy(mask).start()
+    own_far = pltpu.make_async_copy(far_out.at[cube_index()], far_in.at[cube_index()], local_sem.at[0])
+    own_far.start()
+
+    metric_copy.wait_recv()
+    partner = metric_recv[...]
+    own_keys = metric[half:]
+    score_send[0] = dot32(own_keys, partner, NT)
+    own_keys = own_keys.astype(f32)
+    partner = partner.astype(f32)
+    score_send[1] = jnp.broadcast_to(jnp.sum(own_keys * own_keys, axis=1, keepdims=True), (half, LANES))
+    score_send[2] = jnp.broadcast_to(jnp.sum(partner * partner, axis=1, keepdims=True), (half, LANES))
+    score_copy.start()
+
+    own_far.wait()
+    for mask in range(1, 8):
+        far_copy(mask, True).wait_recv()
+    line = iota((rows, rows), 0)
+    turned = ((line // slots) % 8) * 32 + (line // 32) * slots + line % slots
+    turn = (turned == iota((rows, rows), 1)).astype(bf16)
+    near_out[...] = dot32(turn, far_in[...].reshape(rows, part + LANES)).astype(bf16).reshape(near_out.shape)
+    for mask in range(1, 8):
+        near_copy(mask).start()
+    own_near = pltpu.make_async_copy(near_out.at[near_index()], near_in.at[near_index()], local_sem.at[1])
+    own_near.start()
+
+    wanted = iota((rows, LANES), 0) * shards + me
+    from_cube, from_near = cube_and_near(shard_lane)
+    mine = (before <= wanted) & (wanted < before + counts.astype(jnp.int32))
+    fetch = jnp.sum(
+        jnp.where(mine, from_near * 32 + from_cube * slots + ((wanted - before) >> 6), 0), axis=1, keepdims=True
+    )
+    filled = wanted[:, :1] < everyone
+    take = ((fetch == iota((rows, rows), 1)) & filled).astype(bf16)
+    total_ref[...] = jnp.broadcast_to(everyone, total_ref.shape)
+
+    score_copy.wait_recv()
+    sums = score_send[...] + score_recv[...]
+    cosine = sums[0] * lax.rsqrt(sums[1] + epsilon) * to_row(lax.rsqrt(sums[2][:, :1] + epsilon))
+    best_ref[...] = jnp.broadcast_to(to_row(jnp.max(cosine, axis=1, keepdims=True)), best_ref.shape)
+
+    own_near.wait()
+    for mask in range(1, 8):
+        near_copy(mask, True).wait_recv()
+    taken = dot32(take, near_in[...].reshape(rows, part + LANES))
+    half_send[...] = taken[:, :part].astype(bf16)
+    half_copy.start()
+    balanced_ref[:, own_columns] = half_send[...]
+    bias = jnp.where(filled, taken[:, part : part + 1], -9984.0) * LOG2E
+    high = bias.astype(bf16).astype(f32)
+    low = bias - high
+    tile = iota((16, LANES), 0)
+    tiles = jnp.zeros((16, LANES), f32)
+    for i, column in enumerate((high[:half], high[half:], low[:half], low[half:])):
+        tiles = jnp.where(tile == i, to_row(column), tiles)
+    bias_ref[...] = tiles.astype(bf16)
+    half_copy.wait_recv()
+    balanced_ref[:, pl.ds(pl.multiple_of((1 - core) * part, part), part)] = half_recv[...]
+
+    shift.wait_send()
+    metric_copy.wait_send()
+    score_copy.wait_send()
+    half_copy.wait_send()
+    for mask in range(1, 8):
+        counts_to(0, mask).wait_send()
+        counts_to(1, mask).wait_send()
+        far_copy(mask).wait_send()
+        near_copy(mask).wait_send()
+
+
+def deal(tokens, sizes, source, target, count, gain, key_weight):
+    rows, width = tokens.shape
+    half, part = rows // 2, width // 2
+    f32, bf16 = jnp.float32, jnp.bfloat16
+    vmem = pl.BlockSpec(memory_space=pltpu.VMEM)
+    dma = pltpu.SemaphoreType.DMA
+    carried = part + LANES
+    return pl.pallas_call(
+        deal_kernel,
+        in_specs=[vmem, vmem, vmem, vmem, pl.BlockSpec(memory_space=pltpu.SMEM), vmem,
+                  pl.BlockSpec((None, width, key_weight.shape[2]), lambda i: (1, 0, 0))],
+        grid=(1,),
+        out_specs=[vmem] * 4,
+        out_shape=[
+            jax.ShapeDtypeStruct((rows, width), bf16),
+            jax.ShapeDtypeStruct((16, LANES), bf16),
+            jax.ShapeDtypeStruct((8, LANES), jnp.int32),
+            jax.ShapeDtypeStruct((8, LANES), f32),
+        ],
+        scratch_shapes=[
+            pltpu.VMEM((half, carried), bf16),
+            pltpu.VMEM((half, carried), bf16),
+            pltpu.VMEM((2, 8, LANES), f32),
+            pltpu.VMEM((2, 8, 8, LANES), f32),
+            pltpu.VMEM((half, key_weight.shape[2]), bf16),
+            pltpu.VMEM((half, key_weight.shape[2]), bf16),
+            pltpu.VMEM((3, half, LANES), f32),
+            pltpu.VMEM((3, half, LANES), f32),
+            pltpu.VMEM((8, rows // 8, carried), bf16),
+            pltpu.VMEM((8, rows // 8, carried), bf16),
+            pltpu.VMEM((8, rows // 8, carried), bf16),
+            pltpu.VMEM((8, rows // 8, carried), bf16),
+            pltpu.VMEM((rows, part), bf16),
+            pltpu.VMEM((rows, part), bf16),
+            dma((2,)),
+            dma((2, 8)),
+            dma((2, 8)),
+            dma((2,)),
+            dma((2,)),
+            dma((8,)),
+            dma((8,)),
+            dma((8,)),
+            dma((8,)),
+            dma((2,)),
+            dma((2,)),
+        ],
+        compiler_params=pltpu.CompilerParams(
+            vmem_limit_bytes=32 * 2**20, collective_id=8, has_side_effects=True
+        ),
+        cost_estimate=pl.CostEstimate(flops=10**9, bytes_accessed=4 * 2**20, transcendentals=0),
+    )(tokens, sizes, source, target, count, gain, key_weight)
+
+
 def on_device(
     tokens,
     token_sizes,
@@ -377,101 +676,31 @@
     up_weight,
     down_weight,
 ):
+    rows = tokens.shape[0]
+    balanced, bias_tile, grand_total, best = deal(
+        tokens, token_sizes[None, :], merge_source, merge_target, merge_count, attn_gain[None, :], qkv_weight
+    )
+    grand_total = grand_total[0, :1]
     shards = 64
-    me = lax.axis_index(SEQ)
-    rows, width = tokens.shape
-    half = rows // 2
-    slots = rows // shards
-    ids = jnp.arange(half, dtype=jnp.int32)
-    row_ids = jnp.arange(rows, dtype=jnp.int32)
-    shard_ids = jnp.arange(shards, dtype=jnp.int32)
-    ahead = [(i, (i + 1) % shards) for i in range(shards)]
-    behind = [(i, (i - 1) % shards) for i in range(shards)]
-
-    counts = rows - lax.all_gather(merge_count, SEQ, axis=0, tiled=True)
-    active = ids < merge_count[0]
-    hit = (merge_source[0][:, None] == ids[None, :]) & active[:, None]
-    removed = jnp.any(hit, axis=0)
-    goal = jnp.sum(jnp.where(hit, merge_target[0][:, None], 0), axis=0)
-    weights = jnp.where(
-        (goal[None, :] == ids[:, None]) & removed[None, :], token_sizes[half:][None, :], 0
-    ).astype(jnp.bfloat16)
-    merging = lax.ppermute(jnp.concatenate([tokens[half:], weights], axis=1), SEQ, ahead)
-    weights = merging[:, width:]
-    added_rows = dot32(weights, merging[:, :width])
-    added_size = jnp.sum(weights.astype(jnp.float32), axis=1)
-    base_size = token_sizes[:half].astype(jnp.float32)
-    merged = (base_size[:, None] * tokens[:half].astype(jnp.float32) + added_rows) / (
-        base_size + added_size
-    )[:, None]
-    new_rows = jnp.concatenate([merged.astype(jnp.bfloat16), tokens[half:]], axis=0)
-    new_size = jnp.concatenate([base_size + added_size, token_sizes[half:].astype(jnp.float32)])
-    bias_rows = jnp.log(new_size).astype(jnp.bfloat16)
-    bias_lanes = jnp.where(jnp.arange(LANES)[None, :] == 0, bias_rows[:, None], 0).astype(jnp.bfloat16)
-    payload = jnp.concatenate([new_rows, bias_lanes], axis=1)
-
-    survive = jnp.concatenate([jnp.ones((half,), bool), jnp.logical_not(removed)])
-    local_rank = jnp.sum((row_ids[:, None] > row_ids[None, :]) & survive[None, :], axis=1, dtype=jnp.int32)
-    before = jnp.sum(jnp.where(shard_ids[:, None] > shard_ids[None, :], counts[None, :], 0), axis=1)
-    my_start = jnp.sum(jnp.where(shard_ids < me, counts, 0))
-    grand_total = jnp.sum(counts)
-    flat_slot = (my_start + local_rank) % shards * slots + local_rank // shards
-    put = ((flat_slot[None, :] == row_ids[:, None]) & survive[None, :]).astype(jnp.bfloat16)
-    outgoing = dot32(put, payload).astype(jnp.bfloat16).reshape(shards, slots, width + LANES)
-    arrived = lax.all_to_all(outgoing, SEQ, split_axis=0, concat_axis=0, tiled=True)
-    wanted = row_ids * shards + me
-    filled = wanted < grand_total
-    sender = jnp.sum((before[None, :] <= wanted[:, None]).astype(jnp.int32), axis=1) - 1
-    sender_start = jnp.sum(jnp.where(sender[:, None] == shard_ids[None, :], before[None, :], 0), axis=1)
-    fetch = sender * slots + (wanted - sender_start) // shards
-    take = ((fetch[:, None] == row_ids[None, :]) & filled[:, None]).astype(jnp.bfloat16)
-    balanced = dot32(take, arrived.reshape(rows, width + LANES)).astype(jnp.bfloat16)
-    key_bias = jnp.where(filled, balanced[:, width], jnp.bfloat16(empty_bias))
-    balanced = balanced[:, :width]
-
-    bias = key_bias.astype(jnp.float32) * LOG2E
-    high = bias.astype(jnp.bfloat16)
-    low = (bias - high.astype(jnp.float32)).astype(jnp.bfloat16)
-    bias_tile = jnp.concatenate(
-        [high.reshape(2, LANES), low.reshape(2, LANES), jnp.zeros((12, LANES), jnp.bfloat16)], axis=0
-    )
     sizes = (192, 208, rows)
-    needed = (grand_total + shards - 1) // shards
+    needed = (grand_total[0] + shards - 1) // shards
     index = sum((needed > size).astype(jnp.int32) for size in sizes[:-1])
     merged_out = lax.switch(
         index,
         [functools.partial(layer, size, at + 1) for at, size in enumerate(sizes)],
-        grand_total[None], balanced, bias_tile, attn_gain[None, :], mlp_gain[None, :],
+        grand_total, balanced, bias_tile, attn_gain[None, :], mlp_gain[None, :],
         qkv_weight, out_weight, up_weight, down_weight,
     )
-
-    normed = layer_norm(tokens.astype(jnp.float32), attn_gain).astype(jnp.bfloat16)
-    metric = dot32(normed, qkv_weight[1]).astype(jnp.bfloat16)
-    partner = lax.ppermute(metric[:half], SEQ, behind)
-    own_keys = metric[half:]
-    products = dot32(own_keys, partner, NT)
-    own_square = jnp.sum(jnp.square(own_keys.astype(jnp.float32)), axis=1)
-    partner_square = jnp.sum(jnp.square(partner.astype(jnp.float32)), axis=1)
-    sums = jnp.concatenate(
-        [products, jnp.broadcast_to(own_square[:, None], (half, LANES)), jnp.broadcast_to(partner_square[:, None], (half, LANES))], axis=1
-    )
-    sums = sums + swap_cores(sums)
-    cosine = (
-        sums[:, :LANES]
-        * lax.rsqrt(sums[:, LANES] + epsilon)[:, None]
-        * lax.rsqrt(sums[:, 2 * LANES] + epsilon)[None, :]
-    )
-    best_score = jnp.max(cosine, axis=1)
-    return (merged_out, best_score)
+    return (merged_out, best[0])
 
 
 def solution(mesh):
     placed = (
-        P(SEQ, None),
-        P(SEQ),
-        P(SEQ, None),
-        P(SEQ, None),
-        P(SEQ),
+        P("seq", None),
+        P("seq"),
+        P("seq", None),
+        P("seq", None),
+        P("seq"),
         P(),
         P(None, None, "mp"),
         P("mp", None),
@@ -480,5 +709,5 @@
         P("mp", None),
     )
     return jax.shard_map(
-        on_device, mesh=mesh, in_specs=placed, out_specs=(P(SEQ, None), P(SEQ)), check_vma=False
+        on_device, mesh=mesh, in_specs=placed, out_specs=(P("seq", None), P("seq")), check_vma=False
     )

time: 148 us -> 121 us (0.82)
  Pallas kernels: 81.5 us -> 113 us
  starting transfers between devices: 23 us -> 0 us
  blocking collectives: 13.5 us -> 0 us
  waiting for transfers between devices: 11.4 us -> 0 us
  other arithmetic: 7.07 us -> 0 us
  matrix products: 2.89 us -> 0 us
    pallas_call x0 -> x1, Pallas kernels: none -> 35.1 us  [deal(): pl.pallas_call(deal_kernel, in_specs=[vmem, vmem, vmem, vmem, pl.BlockSpe...]
    ppermute x3 -> x0, starting transfers between devices: 15.5 us -> none  [the longest x1 7.27 us: on_device(): partner = lax.ppermute(metric[:half], SEQ, behind)]
    unnamed x1 -> x0, blocking collectives: 13.5 us -> none
    all_to_all x1 -> x0, waiting for transfers between devices: 11.4 us -> none  [on_device(): lax.all_to_all(outgoing, SEQ, split_axis=0, concat_axis=0, tiled=True)]
    all_to_all x1 -> x0, starting transfers between devices: 7.48 us -> none  [on_device(): lax.all_to_all(outgoing, SEQ, split_axis=0, concat_axis=0, tiled=True)]
    pallas_call x1, Pallas kernels: 81.5 us -> 78.4 us  [layer(): pl.pallas_call(functools.partial(layer_kernel, rows, 64 * (total_rows - r...]
    dot_general x5 -> x0, matrix products: 2.89 us -> none  [dot32(): return lax.dot_general(a, b, dims, preferred_element_type=jnp.float32)]
    reduce_sum x11 -> x0, other arithmetic: 2.61 us -> none  [the longest x1 0.8 us: on_device(): goal = jnp.sum(jnp.where(hit, merge_target[0][:, None], 0), axis=0)]
  transfers between devices with their start and end apart: 4 -> 0, of which waited for: 1 -> 0; matrix products, arithmetic and copies ran while one was open for 6% -> 0% of each run, Pallas kernels for 0% -> 0%
where the time goes in v2:
time: 121 us
  Pallas kernels  113 us (93%)
  local copies, waits for them, and re-layouts  4.84 us (4%)
  between operations  1.99 us (2%)
    pallas_call x1, Pallas kernels, layer(): pl.pallas_call(functools.partial(layer_kernel, rows, 64 * (total_rows - r...  78.4 us
    pallas_call x1, Pallas kernels, deal(): pl.pallas_call(deal_kernel, in_specs=[vmem, vmem, vmem, vmem, pl.BlockSpe...  35.1 us
    unnamed x9, local copies, waits for them, and re-layouts  3.82 us

profile of v2, /device:TPU:1, one launch (start us, length us, event | category | flops | bytes accessed | tf_op | source)
XLA Modules:
  0.0 120.5 jit_solution(11107385307309533922)
XLA Ops:
  1.3 0.0 copy-start
  1.3 1.0 copy-done
  2.3 0.0 copy-start.1
  2.3 0.7 copy-done.1
  3.0 0.0 copy-start.2
  3.0 0.7 copy-done.2
  3.7 0.0 copy-start.3
  3.7 0.7 copy-done.3
  4.3 35.1 %shard_map.122 = (bf16[256,1024]{1,0:T(8,128)(2,1)S(1)}, bf16[16,128]{1,0:T(8,128)(2,1)S(1)}, s32[8,128]{1,0:T(8,128)S(1)}, f32[8,128]{1,0:T(8,128)S(1)}) custom-call(bf16[256,1024]{1,0:T(8,128)(2,1)S(1)} %copy-done, s32[1,256]{1,0:T(1,128)S(1)} %bitcast.7, s32[1,128]{1,0:T(1,128)S(1)} %copy-done.2, s32[1,128]{1,0:T(1,128)S(1)} %copy-done.3, ...), custom_call_target="tpu_custom_call" | custom-call | flops 1000000000 | bytes 4194304 | tf_op jit(solution)/shard_map/pallas_call | solution.py:620
  39.4 0.5 slice.6
  40.6 78.7 %conditional.1 = (bf16[256,1024]{1,0:T(8,128)(2,1)S(1)}) conditional(s32[]{:T(128)} %clamp.3, (s32[1]{0:T(128)}, bf16[256,1024]{1,0:T(8,128)(2,1)S(1)}, bf16[16,128]{1,0:T(8,128)(2,1)S(1)}, f32[1,1024]{1,0:T(1,128)}, f32[1,1024]{1,0:T(1,128)}, /*index=5*/bf16[3,1024,512]{2,1,0:T(8,128)(2,1)}, bf16[512,1024]{1,0:T(8,128)(2,1)}, ...), branch_computations={%region_0.1_spmd, %region_1.2_spmd, %region_2.3_spmd} | conditional | flops 8589934592 | bytes 16777224 | solution.py:688
  40.6 78.4 %branch_0_fun.1 = bf16[256,1024]{1,0:T(8,128)(2,1)S(1)} custom-call(s32[1]{0:T(128)} %get-tuple-element.43.total_ref, bf16[256,1024]{1,0:T(8,128)(2,1)S(1)} %get-tuple-element.44.balanced_ref, bf16[16,128]{1,0:T(8,128)(2,1)S(1)} %get-tuple-element.60.bias_ref, f32[1,1024]{1,0:T(1,128)} %get-tuple-element.61.attn_gain_ref, ...), custom_call_target="tpu_custom_call" | custom-call | flops 4831838208 | bytes 16777216 | tf_op jit(solution)/shard_map/cond/branch_0_fun/pallas_call | solution.py:318
  119.2 0.5 slice_bitcast_fusion
  119.8 0.8 copy.18
Async XLA Ops:
  1.3 1.0 copy-start
  2.3 0.7 copy-start.1
  3.0 0.7 copy-start.2
  3.7 0.7 copy-start.3

commit v3 on v2

--- a/solution.py
+++ b/solution.py
@@ -29,7 +29,7 @@
 
 MESH = pl.DeviceIdType.MESH
 ORDERS = ((1, 2, 4), (2, 4, 1), (4, 1, 2))
-PARTS = ((0, 3), (3, 3), (6, 2))
+PARTS = ((0, 3), (3, 3), (6, 3))
 STEP_OF = {0: 0, 1: 1, 2: 2, 4: 3, 3: 4, 5: 5, 6: 6, 7: 7}
 
 
@@ -75,6 +75,7 @@
 def layer_kernel(
     rows,
     dropped,
+    online,
     total_ref,
     balanced_ref,
     bias_ref,
@@ -85,6 +86,7 @@
     up_hbm,
     down_hbm,
     result_ref,
+    plain_ref,
     qkv_w,
     out_w,
     up_w,
@@ -93,6 +95,9 @@
     q_send,
     kv_buf,
     q_buf,
+    tile_send,
+    tile_buf,
+    q_all,
     k2,
     v2,
     acc,
@@ -102,6 +107,8 @@
     part_send,
     part_recv,
     layer_one,
+    norm_send,
+    norm_recv,
     weight_sem,
     local_sem,
     spread_send,
@@ -115,15 +122,15 @@
 ):
     core = lax.axis_index("mp")
     heads = 8
-    block = rows + 16
+    upper = -(-rows // 32) * 16
+    lower = rows - upper
     width = balanced_ref.shape[1]
 
     weight_copies = [
         pltpu.make_async_copy(src, dst, weight_sem.at[i])
         for i, (src, dst) in enumerate(((qkv_hbm, qkv_w), (out_hbm, out_w), (up_hbm, up_w), (down_hbm, down_w)))
     ]
-    for copy in weight_copies:
-        copy.start()
+    weight_copies[0].start()
 
     barrier = pltpu.get_barrier_semaphore()
     for mask in range(1, 8):
@@ -135,14 +142,15 @@
     balanced = balanced_ref[:rows].astype(jnp.float32)
     normed = layer_norm(balanced, attn_gain_ref[...]).astype(jnp.bfloat16)
     weight_copies[0].wait()
+    for copy in weight_copies[1:]:
+        copy.start()
     pl.semaphore_wait(barrier, 11)
 
     key = dot32(normed, qkv_w[1]).astype(jnp.bfloat16)
     value = dot32(normed, qkv_w[2]).astype(jnp.bfloat16)
     for j in range(heads):
         columns = slice(j * HEAD_DIM, (j + 1) * HEAD_DIM)
-        kv_send[j, :rows, :] = jnp.concatenate([key[:, columns], value[:, columns]], axis=1)
-        kv_send[j, rows:, :] = bias_ref[...]
+        kv_send[j] = jnp.concatenate([key[:, columns], value[:, columns]], axis=1)
 
     def spread_kv(mask):
         return pltpu.make_async_remote_copy(
@@ -153,6 +161,12 @@
     def spread_q(mask):
         return pltpu.make_async_remote_copy(
             q_send.at[cube_index(mask)], q_buf.at[mask], spread_send.at[1, mask], spread_recv.at[1, mask],
+            device_id=(far(mask), core), device_id_type=MESH,
+        )
+
+    def spread_tile(mask):
+        return pltpu.make_async_remote_copy(
+            tile_send, tile_buf.at[pl.ds(mask * 16, 16)], spread_send.at[2, mask], spread_recv.at[2, mask],
             device_id=(far(mask), core), device_id_type=MESH,
         )
 
@@ -170,38 +184,95 @@
     own_kv = pltpu.make_async_copy(kv_send.at[cube_index()], kv_buf.at[0, 0], local_sem.at[0])
     own_kv.start()
     query = (dot32(normed, qkv_w[0]) * (HEAD_DIM ** (-0.5) * LOG2E)).astype(jnp.bfloat16)
-    ones = (lax.broadcasted_iota(jnp.int32, (rows, HEAD_DIM), 1) < 2).astype(jnp.bfloat16)
     for j in range(heads):
-        q_send[j] = jnp.concatenate([query[:, j * HEAD_DIM : (j + 1) * HEAD_DIM], ones], axis=1)
+        mine = query[:, j * HEAD_DIM : (j + 1) * HEAD_DIM]
+        other = mine[upper:]
+        if lower < upper:
+            other = jnp.concatenate([other, jnp.zeros((upper - lower, HEAD_DIM), jnp.bfloat16)], axis=0)
+        q_send[j] = jnp.concatenate([mine[:upper], other], axis=1)
     for mask in range(1, 8):
         spread_q(mask).start()
     own_q = pltpu.make_async_copy(q_send.at[cube_index()], q_buf.at[0], local_sem.at[1])
     own_q.start()
+
+    head_of = (
+        iota((heads * HEAD_DIM, LANES), 0) // HEAD_DIM == iota((heads * HEAD_DIM, LANES), 1)
+    ).astype(jnp.bfloat16)
+
+    def widest(values):
+        values = values.astype(jnp.float32)
+        squares = dot32((values * values).astype(jnp.bfloat16), head_of)
+        return jnp.max(jnp.max(squares, axis=1, keepdims=True), axis=0, keepdims=True)
+
+    largest = jnp.max(
+        jnp.max(jnp.abs(value.astype(jnp.float32)), axis=1, keepdims=True), axis=0, keepdims=True
+    )
+    tile = bias_ref[...].astype(jnp.float32)
+    tile_row = iota((16, LANES), 0)
+    for i, bound in ((4, widest(query)), (5, widest(key)), (6, largest)):
+        tile = jnp.where(tile_row == i, jnp.minimum(bound * 1.02, 1e37), tile)
+    tile_send[...] = tile.astype(jnp.bfloat16)
+    for mask in range(1, 8):
+        spread_tile(mask).start()
+    tile_buf[:16] = tile_send[...]
+
     own_kv.wait()
-    own_q.wait()
     for mask in range(1, 8):
         spread_kv(mask).wait_recv()
     for order in range(3):
-        for part in range(3):
+        for part in range(2):
             pass_on(part, ORDERS[part][order], 0).start()
+
+    for mask in range(1, 8):
+        spread_tile(mask).wait_recv()
+    tiles = tile_buf[...]
+    pick_row = iota((8 * 16, LANES), 0)
+    pick_lane = iota((8 * 16, LANES), 1) - HEAD_DIM - pick_row // 16 * 2
+    pick_row = pick_row % 16
+    columns = jnp.concatenate(
+        [
+            dot32(
+                tiles,
+                (((pick_row == i) & (pick_lane == 0)) | ((pick_row == i + 2) & (pick_lane == 1))).astype(jnp.bfloat16),
+                TN,
+            )
+            for i in range(2)
+        ],
+        axis=0,
+    )[:rows]
+    lane = iota((rows, LANES), 1)
+    tiles = tiles.astype(jnp.float32)
+    for i in (4, 5, 6):
+        bound = jnp.max(jnp.where(pick_row == i, tiles, 0.0), axis=0, keepdims=True)
+        columns = jnp.where(lane == 96 + i, bound, columns)
+    kv_buf[0, heads] = columns.astype(jnp.bfloat16)
+    for order in range(3):
+        pass_on(2, ORDERS[2][order], 0).start()
+
+    own_q.wait()
     for mask in range(1, 8):
         spread_q(mask).wait_recv()
-
     queries = heads * rows
     cut = queries // 2 // 256 * 256
+    q_lane = iota((upper, LANES), 1)
+    q_tail = ((q_lane >= HEAD_DIM) & (q_lane < HEAD_DIM + 16)).astype(jnp.bfloat16)
+    for a in range(heads):
+        both = q_buf[a]
+        other = jnp.concatenate([both[:, HEAD_DIM:], q_tail[:, HEAD_DIM:]], axis=1)
+        q_all[a * rows : a * rows + upper, :] = jnp.where(q_lane < HEAD_DIM, both, q_tail)
+        q_all[a * rows + upper : (a + 1) * rows, :] = other[:lower]
+
+    empty = -9984.0 * LOG2E
+    head = jnp.where(
+        iota((8, queries), 0) == 0,
+        float(dropped) if online else float(dropped) * jnp.exp2(jnp.full((8, queries), empty, jnp.float32)),
+        0.0,
+    )
     acc[...] = jnp.zeros_like(acc)
-    empty = -9984.0 * LOG2E
+    acc[:8, :] = head
     peak[...] = jnp.full(peak.shape, empty if dropped else -3e38, jnp.float32)
-    lane = lax.broadcasted_iota(jnp.int32, (rows, LANES), 1)
-    value_tail = (lane == HEAD_DIM).astype(jnp.bfloat16)
-    if dropped:
-        acc[HEAD_DIM : HEAD_DIM + 1, :] = jnp.full((1, queries), float(dropped), jnp.float32)
-    pick_row = lax.broadcasted_iota(jnp.int32, (16, LANES), 0)
-    pick_lane = lax.broadcasted_iota(jnp.int32, (16, LANES), 1)
-    picks = [
-        (((pick_row == i) & (pick_lane == HEAD_DIM)) | ((pick_row == i + 2) & (pick_lane == HEAD_DIM + 1))).astype(jnp.bfloat16)
-        for i in range(2)
-    ]
+    zero = jnp.zeros((), jnp.bfloat16)
+    value_head = (lane == 0).astype(jnp.bfloat16)
 
     def step(i, carry):
         for slot, at in STEP_OF.items():
@@ -219,27 +290,23 @@
                     if came_by != d3:
                         pass_on(part, d3, slot).start()
 
-        def unpack(a, carry):
-            here = pl.ds(pl.multiple_of(a * rows, 16), rows)
-            kv = kv_buf[i, a, :rows, :]
-            tile = kv_buf[i, a, rows:, :]
-            bias = jnp.concatenate(
-                [dot32(tile, picks[0], TN), dot32(tile, picks[1], TN)], axis=0
-            )[:rows].astype(jnp.bfloat16)
-            k2[here, :] = jnp.where(lane < HEAD_DIM, kv, bias)
-            v2[here, :] = jnp.concatenate([kv[:, HEAD_DIM:], value_tail[:, HEAD_DIM:]], axis=1)
-            return carry
-
-        lax.fori_loop(0, heads, unpack, 0)
+        columns = kv_buf[i, heads]
+        for a in range(heads):
+            kv = kv_buf[i, a]
+            bias = jnp.where((lane - HEAD_DIM) // 2 == a, columns, zero)
+            k2[a * rows : (a + 1) * rows, :] = jnp.where(lane < HEAD_DIM, kv, bias)
+            v2[a * rows : (a + 1) * rows, :] = jnp.where(lane < HEAD_DIM, value_head, kv)
         for begin, end in ((0, cut), (cut, queries)):
-            first_a = begin
-            q = q_buf[...].reshape(queries, LANES)[begin:end]
-            s = dot32(k2[...], q, NT)
-            old = peak[:, begin:end]
-            new = jnp.maximum(old, jnp.max(s, axis=0, keepdims=True))
-            p = jnp.exp2(s - new).astype(jnp.bfloat16)
-            peak[:, begin:end] = new
-            acc[:, begin:end] = acc[:, begin:end] * jnp.exp2(old - new) + dot32(v2[...], p, TN)
+            s = dot32(k2[...], q_all[begin:end, :], NT)
+            if online:
+                old = peak[:, begin:end]
+                new = jnp.maximum(old, jnp.max(s, axis=0, keepdims=True))
+                p = jnp.exp2(s - new).astype(jnp.bfloat16)
+                peak[:, begin:end] = new
+                acc[:, begin:end] = acc[:, begin:end] * jnp.exp2(old - new) + dot32(v2[...], p, TN)
+            else:
+                p = jnp.exp2(s).astype(jnp.bfloat16)
+                acc[:, begin:end] += dot32(v2[...], p, TN)
         return carry
 
     lax.fori_loop(0, 8, step, 0)
@@ -256,8 +323,13 @@
             device_id=(far(mask), core), device_id_type=MESH,
         )
 
-    scaled = acc[...] / acc[HEAD_DIM : HEAD_DIM + 1, :]
-    o_send[...] = scaled.T.astype(jnp.bfloat16).reshape(heads, rows, LANES)
+    scaled = (acc[...] / acc[:1, :]).T.astype(jnp.bfloat16)
+    for a in range(heads):
+        first = scaled[a * rows : a * rows + upper, HEAD_DIM:]
+        other = scaled[a * rows + upper : (a + 1) * rows, HEAD_DIM:]
+        if lower < upper:
+            other = jnp.concatenate([other, jnp.zeros((upper - lower, HEAD_DIM), jnp.bfloat16)], axis=0)
+        o_send[a] = jnp.concatenate([first, other], axis=1)
     for mask in range(1, 8):
         back(mask).start()
     own_o = pltpu.make_async_copy(o_send.at[0], o_buf.at[cube_index()], local_sem.at[2])
@@ -273,9 +345,24 @@
             device_id=(lax.axis_index("seq"), 1 - core), device_id_type=MESH,
         )
 
-    mixed = jnp.concatenate([o_buf[j, :, :HEAD_DIM] for j in range(heads)], axis=1)
+    mixed = jnp.concatenate(
+        [
+            jnp.concatenate([o_buf[j, :, :HEAD_DIM] for j in range(heads)], axis=1),
+            jnp.concatenate([o_buf[j, :lower, HEAD_DIM:] for j in range(heads)], axis=1),
+        ],
+        axis=0,
+    )
     part_send[0] = dot32(mixed, out_w[...]).astype(jnp.bfloat16)
     swap(0, rows).start()
+    bounds = kv_buf[0, heads, :16, :].astype(jnp.float32)
+    for i in range(1, 8):
+        bounds = jnp.maximum(bounds, kv_buf[i, heads, :16, :].astype(jnp.float32))
+    norm_send[...] = bounds
+    norm_swap = pltpu.make_async_remote_copy(
+        norm_send, norm_recv, core_send.at[2], core_recv.at[2],
+        device_id=(lax.axis_index("seq"), 1 - core), device_id_type=MESH,
+    )
+    norm_swap.start()
     swap(0, rows).wait_recv()
     attention = part_send[0].astype(jnp.float32) + part_recv[0].astype(jnp.float32)
     layer_one[...] = (balanced_ref[:rows].astype(jnp.float32) + attention).astype(jnp.bfloat16)
@@ -289,6 +376,10 @@
     swap(1, rows).wait_recv()
     mlp = part_send[1].astype(jnp.float32) + part_recv[1].astype(jnp.float32)
     result = layer_one[...].astype(jnp.float32) + mlp
+    norm_swap.wait_recv()
+    bounds = jnp.maximum(norm_send[:8], norm_recv[:8])
+    plain = (bounds[:, 100:101] * bounds[:, 101:102] <= 68.0 * 68.0) & (bounds[:, 102:103] <= 2.0**30)
+    plain_ref[...] = jnp.broadcast_to(jnp.where(plain, 1, 0), plain_ref.shape)
     slot = lax.broadcasted_iota(jnp.int32, (rows, width), 0) * 64 + lax.axis_index("seq")
     result_ref[:rows, :] = jnp.where(slot < total_ref[0], result, 0.0).astype(jnp.bfloat16)
     if rows < result_ref.shape[0]:
@@ -297,6 +388,7 @@
     for mask in range(1, 8):
         spread_kv(mask).wait_send()
         spread_q(mask).wait_send()
+        spread_tile(mask).wait_send()
         back(mask).wait_send()
     for part in range(3):
         d1, d2, d3 = ORDERS[part]
@@ -304,50 +396,60 @@
             pass_on(part, near_mask, slot).wait_send()
     swap(0, rows).wait_send()
     swap(1, rows).wait_send()
-
-
-def layer(rows, which, total, balanced, bias_tile, attn_gain, mlp_gain, qkv_weight, out_weight, up_weight, down_weight):
+    norm_swap.wait_send()
+
+
+def layer(rows, which, online, total, balanced, bias_tile, attn_gain, mlp_gain, qkv_weight, out_weight, up_weight, down_weight):
     total_rows, width = balanced.shape
     heads = 8
     hidden = up_weight.shape[1]
     queries = heads * rows
+    packed = -(-rows // 32) * 16
     bf16 = jnp.bfloat16
     vmem = pl.BlockSpec(memory_space=pltpu.VMEM)
     anywhere = pl.BlockSpec(memory_space=pl.ANY)
     dma = pltpu.SemaphoreType.DMA
     return pl.pallas_call(
-        functools.partial(layer_kernel, rows, 64 * (total_rows - rows)),
+        functools.partial(layer_kernel, rows, 64 * (total_rows - rows), online),
         in_specs=[pl.BlockSpec(memory_space=pltpu.SMEM), vmem, vmem, vmem, vmem] + [anywhere] * 4,
-        out_specs=vmem,
-        out_shape=jax.ShapeDtypeStruct((total_rows, width), bf16),
+        out_specs=[vmem, vmem],
+        out_shape=[
+            jax.ShapeDtypeStruct((total_rows, width), bf16),
+            jax.ShapeDtypeStruct((8, LANES), jnp.int32),
+        ],
         scratch_shapes=[
             pltpu.VMEM(qkv_weight.shape, bf16),
             pltpu.VMEM(out_weight.shape, bf16),
             pltpu.VMEM(up_weight.shape, bf16),
             pltpu.VMEM(down_weight.shape, bf16),
-            pltpu.VMEM((heads, rows + 16, LANES), bf16),
             pltpu.VMEM((heads, rows, LANES), bf16),
-            pltpu.VMEM((8, heads, rows + 16, LANES), bf16),
-            pltpu.VMEM((heads, rows, LANES), bf16),
+            pltpu.VMEM((heads, packed, LANES), bf16),
+            pltpu.VMEM((8, heads + 1, rows, LANES), bf16),
+            pltpu.VMEM((heads, packed, LANES), bf16),
+            pltpu.VMEM((16, LANES), bf16),
+            pltpu.VMEM((8 * 16, LANES), bf16),
+            pltpu.VMEM((queries, LANES), bf16),
             pltpu.VMEM((queries, LANES), bf16),
             pltpu.VMEM((queries, LANES), bf16),
             pltpu.VMEM((LANES, queries), jnp.float32),
             pltpu.VMEM((1, queries), jnp.float32),
-            pltpu.VMEM((heads, rows, LANES), bf16),
-            pltpu.VMEM((heads, rows, LANES), bf16),
+            pltpu.VMEM((heads, packed, LANES), bf16),
+            pltpu.VMEM((heads, packed, LANES), bf16),
             pltpu.VMEM((2, rows, width), bf16),
             pltpu.VMEM((2, rows, width), bf16),
             pltpu.VMEM((rows, width), bf16),
+            pltpu.VMEM((16, LANES), jnp.float32),
+            pltpu.VMEM((16, LANES), jnp.float32),
             dma((4,)),
             dma((3,)),
-            dma((2, 8)),
-            dma((2, 8)),
+            dma((3, 8)),
+            dma((3, 8)),
             dma((3, 8)),
             dma((3, 8)),
             dma((8,)),
             dma((8,)),
-            dma((2,)),
-            dma((2,)),
+            dma((3,)),
+            dma((3,)),
         ],
         compiler_params=pltpu.CompilerParams(
             vmem_limit_bytes=60 * 2**20, collective_id=which, has_side_effects=True
@@ -685,11 +787,15 @@
     sizes = (192, 208, rows)
     needed = (grand_total[0] + shards - 1) // shards
     index = sum((needed > size).astype(jnp.int32) for size in sizes[:-1])
-    merged_out = lax.switch(
-        index,
-        [functools.partial(layer, size, at + 1) for at, size in enumerate(sizes)],
+    operands = (
         grand_total, balanced, bias_tile, attn_gain[None, :], mlp_gain[None, :],
         qkv_weight, out_weight, up_weight, down_weight,
+    )
+    merged_out, plain = lax.switch(
+        index, [functools.partial(layer, size, at + 1, False) for at, size in enumerate(sizes)], *operands
+    )
+    merged_out = lax.cond(
+        plain[0, 0] == 1, lambda done, *_: done, lambda _, *given: layer(rows, 9, True, *given)[0], merged_out, *operands
     )
     return (merged_out, best[0])
 

time: 121 us -> 187 us (1.55)
  Pallas kernels: 113 us -> 178 us
    pallas_call x1 -> x2, Pallas kernels: 78.4 us -> 143 us  [layer(): pl.pallas_call(functools.partial(layer_kernel, rows, 64 * (total_rows - r...]
where the time goes in v3:
time: 187 us; the launch traced here: 186 us
  Pallas kernels  178 us (95%)
  local copies, waits for them, and re-layouts  5.39 us (3%)
  between operations  2.63 us (1%)
    pallas_call x2, Pallas kernels, layer(): pl.pallas_call(functools.partial(layer_kernel, rows, 64 * (total_rows - r...  143 us
    pallas_call x1, Pallas kernels, deal(): pl.pallas_call(deal_kernel, in_specs=[vmem, vmem, vmem, vmem, pl.BlockSpe...  35.1 us
    unnamed x9, local copies, waits for them, and re-layouts  3.82 us

profile of v3, /device:TPU:1, one launch (start us, length us, event | category | flops | bytes accessed | tf_op | source)
XLA Modules:
  0.0 186.1 jit_solution(1001965882143429275)
XLA Ops:
  1.3 0.0 copy-start
  1.3 1.0 copy-done
  2.3 0.0 copy-start.1
  2.3 0.7 copy-done.1
  3.0 0.0 copy-start.2
  3.0 0.7 copy-done.2
  3.7 0.0 copy-start.3
  3.7 0.7 copy-done.3
  4.3 35.1 %shard_map.122 = (bf16[256,1024]{1,0:T(8,128)(2,1)S(1)}, bf16[16,128]{1,0:T(8,128)(2,1)S(1)}, s32[8,128]{1,0:T(8,128)S(1)}, f32[8,128]{1,0:T(8,128)S(1)}) custom-call(bf16[256,1024]{1,0:T(8,128)(2,1)S(1)} %copy-done, s32[1,256]{1,0:T(1,128)S(1)} %bitcast.8, s32[1,128]{1,0:T(1,128)S(1)} %copy-done.2, s32[1,128]{1,0:T(1,128)S(1)} %copy-done.3, ...), custom_call_target="tpu_custom_call" | custom-call | flops 1000000000 | bytes 4194304 | tf_op jit(solution)/shard_map/pallas_call | solution.py:722
  39.4 0.5 slice.9
  40.6 0.5 slice_bitcast_fusion
  41.1 58.2 %conditional.2 = (s32[8,128]{1,0:T(8,128)S(1)}, bf16[256,1024]{1,0:T(8,128)(2,1)S(1)}) conditional(s32[]{:T(128)} %clamp.3, (s32[1]{0:T(128)}, bf16[256,1024]{1,0:T(8,128)(2,1)S(1)}, bf16[16,128]{1,0:T(8,128)(2,1)S(1)}, f32[1,1024]{1,0:T(1,128)}, f32[1,1024]{1,0:T(1,128)}, /*index=5*/bf16[3,1024,512]{2,1,0:T(8,128)(2,1)}, ...), branch_computations={%region_0.1_spmd, %region_1.2_spmd, %region_2.3_spmd} | conditional | flops 8589934592 | bytes 16777232 | solution.py:794
  41.1 58.0 %branch_0_fun.2 = (bf16[256,1024]{1,0:T(8,128)(2,1)S(1)}, s32[8,128]{1,0:T(8,128)S(1)}) custom-call(s32[1]{0:T(128)} %get-tuple-element.83.total_ref, bf16[256,1024]{1,0:T(8,128)(2,1)S(1)} %get-tuple-element.84.balanced_ref, bf16[16,128]{1,0:T(8,128)(2,1)S(1)} %get-tuple-element.85.bias_ref, f32[1,1024]{1,0:T(1,128)} %get-tuple-element.86.attn_gain_ref, ...), custom_call_target="tpu_custom_call" | custom-call | flops 4831838208 | bytes 16777216 | tf_op jit(solution)/shard_map/cond/branch_0_fun/pallas_call | solution.py:412
  99.3 0.5 slice.10
  100.5 84.8 %conditional.3 = (bf16[256,1024]{1,0:T(8,128)(2,1)S(1)}) conditional(s32[]{:T(128)} %bitcast.5, (s32[1]{0:T(128)}, bf16[256,1024]{1,0:T(8,128)(2,1)S(1)}, bf16[16,128]{1,0:T(8,128)(2,1)S(1)}, f32[1,1024]{1,0:T(1,128)}, f32[1,1024]{1,0:T(1,128)}, /*index=5*/bf16[3,1024,512]{2,1,0:T(8,128)(2,1)}, bf16[512,1024]{1,0:T(8,128)(2,1)}, ...), branch_computations={%region_3.4_spmd, %region_4.5_spmd} | conditional | flops 8589934592 | bytes 16777224 | solution.py:797
  100.5 84.8 %branch_0_fun.3 = (bf16[256,1024]{1,0:T(8,128)(2,1)S(1)}, s32[8,128]{1,0:T(8,128)}) custom-call(s32[1]{0:T(128)} %get-tuple-element.116.total_ref, bf16[256,1024]{1,0:T(8,128)(2,1)S(1)} %get-tuple-element.117.balanced_ref, bf16[16,128]{1,0:T(8,128)(2,1)S(1)} %get-tuple-element.118.bias_ref, f32[1,1024]{1,0:T(1,128)} %get-tuple-element.119.attn_gain_ref, ...), custom_call_target="tpu_custom_call" | custom-call | flops 8589934592 | bytes 16777216 | tf_op jit(solution)/shard_map/cond/branch_0_fun/pallas_call | solution.py:412
  185.3 0.8 copy.23
Async XLA Ops:
  1.3 1.0 copy-start
  2.3 0.7 copy-start.1
  3.0 0.7 copy-start.2
  3.7 0.7 copy-start.3

commit v4 on v3

--- a/solution.py
+++ b/solution.py
@@ -29,8 +29,8 @@
 
 MESH = pl.DeviceIdType.MESH
 ORDERS = ((1, 2, 4), (2, 4, 1), (4, 1, 2))
-PARTS = ((0, 3), (3, 3), (6, 3))
-STEP_OF = {0: 0, 1: 1, 2: 2, 4: 3, 3: 4, 5: 5, 6: 6, 7: 7}
+PARTS = ((0, 3), (3, 3), (6, 2))
+CAME = {1: (0, 0), 2: (1, 0), 3: (2, 0), 4: (1, 1), 5: (2, 1), 6: (2, 2), 7: (2, 4)}
 
 
 def places():
@@ -96,7 +96,6 @@
     kv_buf,
     q_buf,
     tile_send,
-    tile_buf,
     q_all,
     k2,
     v2,
@@ -107,6 +106,7 @@
     part_send,
     part_recv,
     layer_one,
+    hidden_buf,
     norm_send,
     norm_recv,
     weight_sem,
@@ -154,7 +154,7 @@
 
     def spread_kv(mask):
         return pltpu.make_async_remote_copy(
-            kv_send.at[cube_index(mask)], kv_buf.at[0, mask], spread_send.at[0, mask], spread_recv.at[0, mask],
+            kv_send.at[cube_index(mask)], kv_buf.at[0, mask, pl.ds(0, rows)], spread_send.at[0, mask], spread_recv.at[0, mask],
             device_id=(far(mask), core), device_id_type=MESH,
         )
 
@@ -166,22 +166,22 @@
 
     def spread_tile(mask):
         return pltpu.make_async_remote_copy(
-            tile_send, tile_buf.at[pl.ds(mask * 16, 16)], spread_send.at[2, mask], spread_recv.at[2, mask],
+            tile_send, kv_buf.at[0, mask, pl.ds(rows, 16)], spread_send.at[2, mask], spread_recv.at[2, mask],
             device_id=(far(mask), core), device_id_type=MESH,
         )
 
-    def pass_on(part, near_mask, slot):
+    def pass_on(part, target):
         first, size = PARTS[part]
-        target = STEP_OF[slot ^ near_mask]
+        order, place = CAME[target]
         return pltpu.make_async_remote_copy(
-            kv_buf.at[STEP_OF[slot], pl.ds(first, size)], kv_buf.at[target, pl.ds(first, size)],
+            kv_buf.at[place, pl.ds(first, size)], kv_buf.at[target, pl.ds(first, size)],
             pass_send.at[part, target], pass_recv.at[part, target],
-            device_id=(near(near_mask), core), device_id_type=MESH,
+            device_id=(near(ORDERS[part][order]), core), device_id_type=MESH,
         )
 
     for mask in range(1, 8):
         spread_kv(mask).start()
-    own_kv = pltpu.make_async_copy(kv_send.at[cube_index()], kv_buf.at[0, 0], local_sem.at[0])
+    own_kv = pltpu.make_async_copy(kv_send.at[cube_index()], kv_buf.at[0, 0, pl.ds(0, rows)], local_sem.at[0])
     own_kv.start()
     query = (dot32(normed, qkv_w[0]) * (HEAD_DIM ** (-0.5) * LOG2E)).astype(jnp.bfloat16)
     for j in range(heads):
@@ -214,40 +214,24 @@
     tile_send[...] = tile.astype(jnp.bfloat16)
     for mask in range(1, 8):
         spread_tile(mask).start()
-    tile_buf[:16] = tile_send[...]
+    kv_buf[0, 0, rows:, :] = tile_send[...]
 
     own_kv.wait()
     for mask in range(1, 8):
         spread_kv(mask).wait_recv()
-    for order in range(3):
-        for part in range(2):
-            pass_on(part, ORDERS[part][order], 0).start()
-
-    for mask in range(1, 8):
         spread_tile(mask).wait_recv()
-    tiles = tile_buf[...]
+    for target in (1, 2, 3):
+        for part in range(3):
+            pass_on(part, target).start()
+
     pick_row = iota((8 * 16, LANES), 0)
     pick_lane = iota((8 * 16, LANES), 1) - HEAD_DIM - pick_row // 16 * 2
     pick_row = pick_row % 16
-    columns = jnp.concatenate(
-        [
-            dot32(
-                tiles,
-                (((pick_row == i) & (pick_lane == 0)) | ((pick_row == i + 2) & (pick_lane == 1))).astype(jnp.bfloat16),
-                TN,
-            )
-            for i in range(2)
-        ],
-        axis=0,
-    )[:rows]
+    picks = [
+        (((pick_row == i) & (pick_lane == 0)) | ((pick_row == i + 2) & (pick_lane == 1))).astype(jnp.bfloat16)
+        for i in range(2)
+    ]
     lane = iota((rows, LANES), 1)
-    tiles = tiles.astype(jnp.float32)
-    for i in (4, 5, 6):
-        bound = jnp.max(jnp.where(pick_row == i, tiles, 0.0), axis=0, keepdims=True)
-        columns = jnp.where(lane == 96 + i, bound, columns)
-    kv_buf[0, heads] = columns.astype(jnp.bfloat16)
-    for order in range(3):
-        pass_on(2, ORDERS[2][order], 0).start()
 
     own_q.wait()
     for mask in range(1, 8):
@@ -275,24 +259,21 @@
     value_head = (lane == 0).astype(jnp.bfloat16)
 
     def step(i, carry):
-        for slot, at in STEP_OF.items():
-            if slot == 0:
-                continue
-
-            @pl.when(i == at)
-            def _(slot=slot):
+        for place in CAME:
+
+            @pl.when(i == place)
+            def _(place=place):
                 for part in range(3):
-                    d1, d2, d3 = ORDERS[part]
-                    came_by = d3 if slot & d3 else d2 if slot & d2 else d1
-                    pass_on(part, came_by, slot ^ came_by).wait_recv()
-                    if came_by == d1:
-                        pass_on(part, d2, slot).start()
-                    if came_by != d3:
-                        pass_on(part, d3, slot).start()
-
-        columns = kv_buf[i, heads]
+                    pass_on(part, place).wait_recv()
+                for target, (_, start) in CAME.items():
+                    if start == place:
+                        for part in range(3):
+                            pass_on(part, target).start()
+
+        tiles = kv_buf[i, :, rows:, :].reshape(8 * 16, LANES)
+        columns = jnp.concatenate([dot32(tiles, pick, TN) for pick in picks], axis=0)[:rows].astype(jnp.bfloat16)
         for a in range(heads):
-            kv = kv_buf[i, a]
+            kv = kv_buf[i, a, :rows, :]
             bias = jnp.where((lane - HEAD_DIM) // 2 == a, columns, zero)
             k2[a * rows : (a + 1) * rows, :] = jnp.where(lane < HEAD_DIM, kv, bias)
             v2[a * rows : (a + 1) * rows, :] = jnp.where(lane < HEAD_DIM, value_head, kv)
@@ -339,10 +320,22 @@
     for mask in range(1, 8):
         back_in(mask).wait_recv()
 
-    def swap(which, size):
+    def swap(which, piece):
         return pltpu.make_async_remote_copy(
-            part_send.at[which], part_recv.at[which], core_send.at[which], core_recv.at[which],
+            part_send.at[which, piece], part_recv.at[which, piece],
+            core_send.at[2 * which + piece], core_recv.at[2 * which + piece],
             device_id=(lax.axis_index("seq"), 1 - core), device_id_type=MESH,
+        )
+
+    half = width // 2
+
+    def both(which):
+        return jnp.concatenate(
+            [
+                part_send[which, piece].astype(jnp.float32) + part_recv[which, piece].astype(jnp.float32)
+                for piece in range(2)
+            ],
+            axis=1,
         )
 
     mixed = jnp.concatenate(
@@ -352,34 +345,39 @@
         ],
         axis=0,
     )
-    part_send[0] = dot32(mixed, out_w[...]).astype(jnp.bfloat16)
-    swap(0, rows).start()
-    bounds = kv_buf[0, heads, :16, :].astype(jnp.float32)
-    for i in range(1, 8):
-        bounds = jnp.maximum(bounds, kv_buf[i, heads, :16, :].astype(jnp.float32))
+    for piece in range(2):
+        part_send[0, piece] = dot32(mixed, out_w[:, piece * half : (piece + 1) * half]).astype(jnp.bfloat16)
+        swap(0, piece).start()
+    bounds = jnp.max(kv_buf[:, :, rows:, :].reshape(8 * heads, 16, LANES).astype(jnp.float32), axis=0)
     norm_send[...] = bounds
     norm_swap = pltpu.make_async_remote_copy(
-        norm_send, norm_recv, core_send.at[2], core_recv.at[2],
+        norm_send, norm_recv, core_send.at[4], core_recv.at[4],
         device_id=(lax.axis_index("seq"), 1 - core), device_id_type=MESH,
     )
     norm_swap.start()
-    swap(0, rows).wait_recv()
-    attention = part_send[0].astype(jnp.float32) + part_recv[0].astype(jnp.float32)
+    swap(0, 0).wait_recv()
+    swap(0, 1).wait_recv()
+    attention = both(0)
     layer_one[...] = (balanced_ref[:rows].astype(jnp.float32) + attention).astype(jnp.bfloat16)
     normed_mlp = layer_norm(layer_one[...].astype(jnp.float32), mlp_gain_ref[...]).astype(jnp.bfloat16)
     weight_copies[2].wait()
     weight_copies[3].wait()
-    hidden = dot32(normed_mlp, up_w[...])
-    hidden = (0.5 * hidden * (1.0 + lax.erf(hidden * math.sqrt(0.5)))).astype(jnp.bfloat16)
-    part_send[1] = dot32(hidden, down_w[...]).astype(jnp.bfloat16)
-    swap(1, rows).start()
-    swap(1, rows).wait_recv()
-    mlp = part_send[1].astype(jnp.float32) + part_recv[1].astype(jnp.float32)
+    step_width = up_w.shape[1] // 4
+    for piece in range(4):
+        columns = slice(piece * step_width, (piece + 1) * step_width)
+        hidden = dot32(normed_mlp, up_w[:, columns])
+        hidden_buf[:, columns] = (0.5 * hidden * (1.0 + lax.erf(hidden * math.sqrt(0.5)))).astype(jnp.bfloat16)
+    for piece in range(2):
+        part_send[1, piece] = dot32(hidden_buf[...], down_w[:, piece * half : (piece + 1) * half]).astype(jnp.bfloat16)
+        swap(1, piece).start()
+    norm_swap.wait_recv()
+    bounds = jnp.maximum(norm_send[...], norm_recv[...])
+    plain = (bounds[4:5] * bounds[5:6] <= 68.0 * 68.0) & (bounds[6:7] <= 2.0**30)
+    plain_ref[0] = jnp.min(jnp.where(plain, 1, 0))
+    swap(1, 0).wait_recv()
+    swap(1, 1).wait_recv()
+    mlp = both(1)
     result = layer_one[...].astype(jnp.float32) + mlp
-    norm_swap.wait_recv()
-    bounds = jnp.maximum(norm_send[:8], norm_recv[:8])
-    plain = (bounds[:, 100:101] * bounds[:, 101:102] <= 68.0 * 68.0) & (bounds[:, 102:103] <= 2.0**30)
-    plain_ref[...] = jnp.broadcast_to(jnp.where(plain, 1, 0), plain_ref.shape)
     slot = lax.broadcasted_iota(jnp.int32, (rows, width), 0) * 64 + lax.axis_index("seq")
     result_ref[:rows, :] = jnp.where(slot < total_ref[0], result, 0.0).astype(jnp.bfloat16)
     if rows < result_ref.shape[0]:
@@ -391,11 +389,11 @@
         spread_tile(mask).wait_send()
         back(mask).wait_send()
     for part in range(3):
-        d1, d2, d3 = ORDERS[part]
-        for near_mask, slot in ((d1, 0), (d2, 0), (d3, 0), (d2, d1), (d3, d1), (d3, d2), (d3, d1 | d2)):
-            pass_on(part, near_mask, slot).wait_send()
-    swap(0, rows).wait_send()
-    swap(1, rows).wait_send()
+        for target in CAME:
+            pass_on(part, target).wait_send()
+    for which in range(2):
+        swap(which, 0).wait_send()
+        swap(which, 1).wait_send()
     norm_swap.wait_send()
 
 
@@ -412,10 +410,10 @@
     return pl.pallas_call(
         functools.partial(layer_kernel, rows, 64 * (total_rows - rows), online),
         in_specs=[pl.BlockSpec(memory_space=pltpu.SMEM), vmem, vmem, vmem, vmem] + [anywhere] * 4,
-        out_specs=[vmem, vmem],
+        out_specs=[vmem, pl.BlockSpec(memory_space=pltpu.SMEM)],
         out_shape=[
             jax.ShapeDtypeStruct((total_rows, width), bf16),
-            jax.ShapeDtypeStruct((8, LANES), jnp.int32),
+            jax.ShapeDtypeStruct((1,), jnp.int32),
         ],
         scratch_shapes=[
             pltpu.VMEM(qkv_weight.shape, bf16),
@@ -424,10 +422,9 @@
             pltpu.VMEM(down_weight.shape, bf16),
             pltpu.VMEM((heads, rows, LANES), bf16),
             pltpu.VMEM((heads, packed, LANES), bf16),
-            pltpu.VMEM((8, heads + 1, rows, LANES), bf16),
+            pltpu.VMEM((8, heads, rows + 16, LANES), bf16),
             pltpu.VMEM((heads, packed, LANES), bf16),
             pltpu.VMEM((16, LANES), bf16),
-            pltpu.VMEM((8 * 16, LANES), bf16),
             pltpu.VMEM((queries, LANES), bf16),
             pltpu.VMEM((queries, LANES), bf16),
             pltpu.VMEM((queries, LANES), bf16),
@@ -435,9 +432,10 @@
             pltpu.VMEM((1, queries), jnp.float32),
             pltpu.VMEM((heads, packed, LANES), bf16),
             pltpu.VMEM((heads, packed, LANES), bf16),
-            pltpu.VMEM((2, rows, width), bf16),
-            pltpu.VMEM((2, rows, width), bf16),
+            pltpu.VMEM((2, 2, rows, width // 2), bf16),
+            pltpu.VMEM((2, 2, rows, width // 2), bf16),
             pltpu.VMEM((rows, width), bf16),
+            pltpu.VMEM((rows, hidden), bf16),
             pltpu.VMEM((16, LANES), jnp.float32),
             pltpu.VMEM((16, LANES), jnp.float32),
             dma((4,)),
@@ -448,8 +446,8 @@
             dma((3, 8)),
             dma((8,)),
             dma((8,)),
-            dma((3,)),
-            dma((3,)),
+            dma((5,)),
+            dma((5,)),
         ],
         compiler_params=pltpu.CompilerParams(
             vmem_limit_bytes=60 * 2**20, collective_id=which, has_side_effects=True
@@ -489,17 +487,25 @@
 
 
 def deal_kernel(
+    choices,
+    tokens_hbm,
+    sizes_hbm,
+    source_hbm,
+    target_hbm,
+    count_ref,
+    gain_ref,
+    qkv_hbm,
+    balanced_ref,
+    bias_ref,
+    total_ref,
+    index_ref,
+    best_ref,
     tokens_ref,
     sizes_ref,
     source_ref,
     target_ref,
-    count_ref,
-    gain_ref,
     key_w,
-    balanced_ref,
-    bias_ref,
-    total_ref,
-    best_ref,
+    metric,
     shift_send,
     shift_recv,
     count_send,
@@ -525,6 +531,7 @@
     near_recv_sem,
     half_sem,
     local_sem,
+    load_sem,
 ):
     me = lax.axis_index("seq")
     core = lax.axis_index("mp")
@@ -537,6 +544,20 @@
     own_columns = pl.ds(pl.multiple_of(core * part, part), part)
     f32, bf16 = jnp.float32, jnp.bfloat16
 
+    loads = [
+        pltpu.make_async_copy(src, dst, load_sem.at[i])
+        for i, (src, dst) in enumerate(
+            (
+                (sizes_hbm, sizes_ref),
+                (source_hbm, source_ref),
+                (target_hbm, target_ref),
+                (tokens_hbm, tokens_ref),
+                (qkv_hbm.at[1], key_w),
+            )
+        )
+    ]
+    for load in loads:
+        load.start()
     barrier = pltpu.get_barrier_semaphore()
     for mask in range(1, 8):
         pl.semaphore_signal(barrier, inc=1, device_id=(far(mask), core), device_id_type=MESH)
@@ -573,6 +594,8 @@
             near_send_sem.at[mask], near_recv_sem.at[mask], near(mask), core,
         )
 
+    for load in loads[:4]:
+        load.wait()
     count = count_ref[0]
     active = iota((1, half), 1) < count
     hit = (source_ref[...] == iota((half, half), 0)) & active
@@ -589,11 +612,6 @@
     shift.start()
     for mask in range(1, 8):
         counts_to(0, mask).start()
-
-    normed = layer_norm(tokens_ref[...].astype(f32), gain_ref[...]).astype(bf16)
-    metric = dot32(normed, key_w[...]).astype(bf16)
-    metric_send[...] = metric[:half]
-    metric_copy.start()
 
     for mask in range(1, 8):
         counts_to(0, mask).wait_recv()
@@ -646,6 +664,36 @@
     own_far = pltpu.make_async_copy(far_out.at[cube_index()], far_in.at[cube_index()], local_sem.at[0])
     own_far.start()
 
+    normed = layer_norm(tokens_ref[...].astype(f32), gain_ref[...]).astype(bf16)
+    loads[4].wait()
+    metric[...] = dot32(normed, key_w[...]).astype(bf16)
+    metric_send[...] = metric[:half]
+    metric_copy.start()
+    own_far.wait()
+    for mask in range(1, 8):
+        far_copy(mask, True).wait_recv()
+    line = iota((rows, rows), 0)
+    turned = ((line // slots) % 8) * 32 + (line // 32) * slots + line % slots
+    turn = (turned == iota((rows, rows), 1)).astype(bf16)
+    near_out[...] = dot32(turn, far_in[...].reshape(rows, part + LANES)).astype(bf16).reshape(near_out.shape)
+    for mask in range(1, 8):
+        near_copy(mask).start()
+    own_near = pltpu.make_async_copy(near_out.at[near_index()], near_in.at[near_index()], local_sem.at[1])
+    own_near.start()
+
+    wanted = iota((rows, LANES), 0) * shards + me
+    from_cube, from_near = cube_and_near(shard_lane)
+    mine = (before <= wanted) & (wanted < before + counts.astype(jnp.int32))
+    fetch = jnp.sum(
+        jnp.where(mine, from_near * 32 + from_cube * slots + ((wanted - before) >> 6), 0), axis=1, keepdims=True
+    )
+    filled = wanted[:, :1] < everyone
+    take = ((fetch == iota((rows, rows), 1)) & filled).astype(bf16)
+    everything = jnp.sum(counts.astype(jnp.int32))
+    total_ref[0] = everything
+    needed = (everything + shards - 1) >> 6
+    index_ref[0] = sum((needed > size).astype(jnp.int32) for size in choices[:-1])
+
     metric_copy.wait_recv()
     partner = metric_recv[...]
     own_keys = metric[half:]
@@ -655,33 +703,6 @@
     score_send[1] = jnp.broadcast_to(jnp.sum(own_keys * own_keys, axis=1, keepdims=True), (half, LANES))
     score_send[2] = jnp.broadcast_to(jnp.sum(partner * partner, axis=1, keepdims=True), (half, LANES))
     score_copy.start()
-
-    own_far.wait()
-    for mask in range(1, 8):
-        far_copy(mask, True).wait_recv()
-    line = iota((rows, rows), 0)
-    turned = ((line // slots) % 8) * 32 + (line // 32) * slots + line % slots
-    turn = (turned == iota((rows, rows), 1)).astype(bf16)
-    near_out[...] = dot32(turn, far_in[...].reshape(rows, part + LANES)).astype(bf16).reshape(near_out.shape)
-    for mask in range(1, 8):
-        near_copy(mask).start()
-    own_near = pltpu.make_async_copy(near_out.at[near_index()], near_in.at[near_index()], local_sem.at[1])
-    own_near.start()
-
-    wanted = iota((rows, LANES), 0) * shards + me
-    from_cube, from_near = cube_and_near(shard_lane)
-    mine = (before <= wanted) & (wanted < before + counts.astype(jnp.int32))
-    fetch = jnp.sum(
-        jnp.where(mine, from_near * 32 + from_cube * slots + ((wanted - before) >> 6), 0), axis=1, keepdims=True
-    )
-    filled = wanted[:, :1] < everyone
-    take = ((fetch == iota((rows, rows), 1)) & filled).astype(bf16)
-    total_ref[...] = jnp.broadcast_to(everyone, total_ref.shape)
-
-    score_copy.wait_recv()
-    sums = score_send[...] + score_recv[...]
-    cosine = sums[0] * lax.rsqrt(sums[1] + epsilon) * to_row(lax.rsqrt(sums[2][:, :1] + epsilon))
-    best_ref[...] = jnp.broadcast_to(to_row(jnp.max(cosine, axis=1, keepdims=True)), best_ref.shape)
 
     own_near.wait()
     for mask in range(1, 8):
@@ -698,6 +719,10 @@
     for i, column in enumerate((high[:half], high[half:], low[:half], low[half:])):
         tiles = jnp.where(tile == i, to_row(column), tiles)
     bias_ref[...] = tiles.astype(bf16)
+    score_copy.wait_recv()
+    sums = score_send[...] + score_recv[...]
+    cosine = sums[0] * lax.rsqrt(sums[1] + epsilon) * to_row(lax.rsqrt(sums[2][:, :1] + epsilon))
+    best_ref[...] = to_row(jnp.max(cosine, axis=1, keepdims=True))
     half_copy.wait_recv()
     balanced_ref[:, pl.ds(pl.multiple_of((1 - core) * part, part), part)] = half_recv[...]
 
@@ -712,32 +737,40 @@
         near_copy(mask).wait_send()
 
 
-def deal(tokens, sizes, source, target, count, gain, key_weight):
+def deal(choices, tokens, sizes, source, target, count, gain, qkv_weight):
     rows, width = tokens.shape
     half, part = rows // 2, width // 2
     f32, bf16 = jnp.float32, jnp.bfloat16
     vmem = pl.BlockSpec(memory_space=pltpu.VMEM)
     dma = pltpu.SemaphoreType.DMA
     carried = part + LANES
+    hbm = pl.BlockSpec(memory_space=pltpu.HBM)
+    smem = pl.BlockSpec(memory_space=pltpu.SMEM)
+    local_width = qkv_weight.shape[2]
     return pl.pallas_call(
-        deal_kernel,
-        in_specs=[vmem, vmem, vmem, vmem, pl.BlockSpec(memory_space=pltpu.SMEM), vmem,
-                  pl.BlockSpec((None, width, key_weight.shape[2]), lambda i: (1, 0, 0))],
-        grid=(1,),
-        out_specs=[vmem] * 4,
+        functools.partial(deal_kernel, choices),
+        in_specs=[hbm, hbm, hbm, hbm, smem, vmem, hbm],
+        out_specs=[vmem, vmem, smem, smem, vmem],
         out_shape=[
             jax.ShapeDtypeStruct((rows, width), bf16),
             jax.ShapeDtypeStruct((16, LANES), bf16),
-            jax.ShapeDtypeStruct((8, LANES), jnp.int32),
-            jax.ShapeDtypeStruct((8, LANES), f32),
+            jax.ShapeDtypeStruct((1,), jnp.int32),
+            jax.ShapeDtypeStruct((1,), jnp.int32),
+            jax.ShapeDtypeStruct((1, half), f32),
         ],
         scratch_shapes=[
+            pltpu.VMEM((rows, width), bf16),
+            pltpu.VMEM((1, rows), jnp.int32),
+            pltpu.VMEM((1, half), jnp.int32),
+            pltpu.VMEM((1, half), jnp.int32),
+            pltpu.VMEM((width, local_width), bf16),
+            pltpu.VMEM((rows, local_width), bf16),
             pltpu.VMEM((half, carried), bf16),
             pltpu.VMEM((half, carried), bf16),
             pltpu.VMEM((2, 8, LANES), f32),
             pltpu.VMEM((2, 8, 8, LANES), f32),
-            pltpu.VMEM((half, key_weight.shape[2]), bf16),
-            pltpu.VMEM((half, key_weight.shape[2]), bf16),
+            pltpu.VMEM((half, local_width), bf16),
+            pltpu.VMEM((half, local_width), bf16),
             pltpu.VMEM((3, half, LANES), f32),
             pltpu.VMEM((3, half, LANES), f32),
             pltpu.VMEM((8, rows // 8, carried), bf16),
@@ -757,12 +790,13 @@
             dma((8,)),
             dma((2,)),
             dma((2,)),
+            dma((5,)),
         ],
         compiler_params=pltpu.CompilerParams(
             vmem_limit_bytes=32 * 2**20, collective_id=8, has_side_effects=True
         ),
         cost_estimate=pl.CostEstimate(flops=10**9, bytes_accessed=4 * 2**20, transcendentals=0),
-    )(tokens, sizes, source, target, count, gain, key_weight)
+    )(tokens, sizes, source, target, count, gain, qkv_weight)
 
 
 def on_device(
@@ -779,23 +813,19 @@
     down_weight,
 ):
     rows = tokens.shape[0]
-    balanced, bias_tile, grand_total, best = deal(
-        tokens, token_sizes[None, :], merge_source, merge_target, merge_count, attn_gain[None, :], qkv_weight
-    )
-    grand_total = grand_total[0, :1]
-    shards = 64
     sizes = (192, 208, rows)
-    needed = (grand_total[0] + shards - 1) // shards
-    index = sum((needed > size).astype(jnp.int32) for size in sizes[:-1])
+    balanced, bias_tile, grand_total, index, best = deal(
+        sizes, tokens, token_sizes[None, :], merge_source, merge_target, merge_count, attn_gain[None, :], qkv_weight
+    )
     operands = (
         grand_total, balanced, bias_tile, attn_gain[None, :], mlp_gain[None, :],
         qkv_weight, out_weight, up_weight, down_weight,
     )
     merged_out, plain = lax.switch(
-        index, [functools.partial(layer, size, at + 1, False) for at, size in enumerate(sizes)], *operands
+        index[0], [functools.partial(layer, size, at + 1, False) for at, size in enumerate(sizes)], *operands
     )
     merged_out = lax.cond(
-        plain[0, 0] == 1, lambda done, *_: done, lambda _, *given: layer(rows, 9, True, *given)[0], merged_out, *operands
+        plain[0] == 1, lambda done, *_: done, lambda _, *given: layer(rows, 9, True, *given)[0], merged_out, *operands
     )
     return (merged_out, best[0])
 

time: 187 us -> 182 us (0.973)
  Pallas kernels: 178 us -> 175 us
    pallas_call x2, Pallas kernels: 143 us -> 139 us  [layer(): pl.pallas_call(functools.partial(layer_kernel, rows, 64 * (total_rows - r...]
    unnamed x9 -> x10, local copies, waits for them, and re-layouts: 3.82 us -> 4.33 us
where the time goes in v4:
time: 182 us
  Pallas kernels  175 us (96%)
  local copies, waits for them, and re-layouts  4.33 us (2%)
  between operations  2.56 us (1%)
    pallas_call x2, Pallas kernels, layer(): pl.pallas_call(functools.partial(layer_kernel, rows, 64 * (total_rows - r...  139 us
    pallas_call x1, Pallas kernels, deal(): pl.pallas_call(functools.partial(deal_kernel, choices), in_specs=[hbm, hb...  35.2 us
    unnamed x10, local copies, waits for them, and re-layouts  4.33 us

profile of v4, /device:TPU:1, one launch (start us, length us, event | category | flops | bytes accessed | tf_op | source)
XLA Modules:
  0.0 181.6 jit_solution(15090097908469884061)
XLA Ops:
  1.3 0.0 copy-start
  1.3 1.0 copy-done
  2.3 0.0 copy-start.1
  2.3 0.7 copy-done.1
  3.0 0.0 copy-start.2
  3.0 0.7 copy-done.2
  3.7 0.0 copy-start.3
  3.7 0.7 copy-done.3
  4.3 35.2 %shard_map.122 = (bf16[256,1024]{1,0:T(8,128)(2,1)S(1)}, bf16[16,128]{1,0:T(8,128)(2,1)S(1)}, s32[1]{0:T(128)}, s32[1]{0:T(128)}, f32[1,128]{1,0:T(1,128)S(1)}) custom-call(bf16[256,1024]{1,0:T(8,128)(2,1)S(1)} %copy-done, s32[1,256]{1,0:T(1,128)S(1)} %bitcast.6, s32[1,128]{1,0:T(1,128)S(1)} %copy-done.2, s32[1,128]{1,0:T(1,128)S(1)} %copy-done.3, ...), custom_call_target="tpu_custom_call" | custom-call | flops 1000000000 | bytes 4194304 | tf_op jit(solution)/shard_map/pallas_call | solution.py:750
  40.2 55.4 %conditional.2 = (s32[1]{0:T(128)}, bf16[256,1024]{1,0:T(8,128)(2,1)S(1)}) conditional(s32[]{:T(128)} %bitcast.2, (s32[1]{0:T(128)}, bf16[256,1024]{1,0:T(8,128)(2,1)S(1)}, bf16[16,128]{1,0:T(8,128)(2,1)S(1)}, f32[1,1024]{1,0:T(1,128)}, f32[1,1024]{1,0:T(1,128)}, /*index=5*/bf16[3,1024,512]{2,1,0:T(8,128)(2,1)}, ...), branch_computations={%region_0.0_spmd, %region_1.0_spmd, %region_2.0_spmd} | conditional | flops 8589934592 | bytes 16777232 | solution.py:824
  40.2 55.3 %branch_0_fun.2 = (bf16[256,1024]{1,0:T(8,128)(2,1)S(1)}, s32[1]{0:T(128)}) custom-call(s32[1]{0:T(128)} %get-tuple-element.83.total_ref, bf16[256,1024]{1,0:T(8,128)(2,1)S(1)} %get-tuple-element.84.balanced_ref, bf16[16,128]{1,0:T(8,128)(2,1)S(1)} %get-tuple-element.85.bias_ref, f32[1,1024]{1,0:T(1,128)} %get-tuple-element.86.attn_gain_ref, ...), custom_call_target="tpu_custom_call" | custom-call | flops 4831838208 | bytes 16777216 | tf_op jit(solution)/shard_map/cond/branch_0_fun/pallas_call | solution.py:410
  96.2 84.1 %conditional.3 = (bf16[256,1024]{1,0:T(8,128)(2,1)S(1)}) conditional(s32[]{:T(128)} %bitcast.4, (s32[1]{0:T(128)}, bf16[256,1024]{1,0:T(8,128)(2,1)S(1)}, bf16[16,128]{1,0:T(8,128)(2,1)S(1)}, f32[1,1024]{1,0:T(1,128)}, f32[1,1024]{1,0:T(1,128)}, /*index=5*/bf16[3,1024,512]{2,1,0:T(8,128)(2,1)}, bf16[512,1024]{1,0:T(8,128)(2,1)}, ...), branch_computations={%region_3.0_spmd, %region_4.0_spmd} | conditional | flops 8589934592 | bytes 16777224 | solution.py:827
  96.2 84.1 %branch_0_fun.3 = (bf16[256,1024]{1,0:T(8,128)(2,1)S(1)}, s32[1]{0:T(128)}) custom-call(s32[1]{0:T(128)} %get-tuple-element.116.total_ref, bf16[256,1024]{1,0:T(8,128)(2,1)S(1)} %get-tuple-element.117.balanced_ref, bf16[16,128]{1,0:T(8,128)(2,1)S(1)} %get-tuple-element.118.bias_ref, f32[1,1024]{1,0:T(1,128)} %get-tuple-element.119.attn_gain_ref, ...), custom_call_target="tpu_custom_call" | custom-call | flops 8589934592 | bytes 16777216 | tf_op jit(solution)/shard_map/cond/branch_0_fun/pallas_call | solution.py:410
  180.3 0.8 copy.24
  181.1 0.5 copy.25
Async XLA Ops:
  1.3 1.0 copy-start
  2.3 0.7 copy-start.1
  3.0 0.7 copy-start.2
  3.7 0.7 copy-start.3

commit v5 on v4

--- a/solution.py
+++ b/solution.py
@@ -793,7 +793,7 @@
             dma((5,)),
         ],
         compiler_params=pltpu.CompilerParams(
-            vmem_limit_bytes=32 * 2**20, collective_id=8, has_side_effects=True
+            vmem_limit_bytes=62 * 2**20, collective_id=8, has_side_effects=True
         ),
         cost_estimate=pl.CostEstimate(flops=10**9, bytes_accessed=4 * 2**20, transcendentals=0),
     )(tokens, sizes, source, target, count, gain, qkv_weight)
@@ -813,7 +813,7 @@
     down_weight,
 ):
     rows = tokens.shape[0]
-    sizes = (192, 208, rows)
+    sizes = (208, rows)
     balanced, bias_tile, grand_total, index, best = deal(
         sizes, tokens, token_sizes[None, :], merge_source, merge_target, merge_count, attn_gain[None, :], qkv_weight
     )

time: 182 us -> 182 us (level)
  local copies, waits for them, and re-layouts: 4.33 us -> 1.31 us
  Pallas kernels: 175 us -> 178 us
    pallas_call x2, Pallas kernels: 139 us -> 143 us  [layer(): pl.pallas_call(functools.partial(layer_kernel, rows, 64 * (total_rows - r...]
    unnamed x10 -> x4, local copies, waits for them, and re-layouts: 4.33 us -> 1.31 us
where the time goes in v5:
time: 182 us
  Pallas kernels  178 us (98%)
  between operations  2.55 us (1%)
    pallas_call x2, Pallas kernels, layer(): pl.pallas_call(functools.partial(layer_kernel, rows, 64 * (total_rows - r...  143 us
    pallas_call x1, Pallas kernels, deal(): pl.pallas_call(functools.partial(deal_kernel, choices), in_specs=[hbm, hb...  35.1 us

profile of v5, /device:TPU:1, one launch (start us, length us, event | category | flops | bytes accessed | tf_op | source)
XLA Modules:
  0.0 182.1 jit_solution(1943586021483454193)
XLA Ops:
  1.3 35.1 %shard_map.122 = (bf16[256,1024]{1,0:T(8,128)(2,1)S(1)}, bf16[16,128]{1,0:T(8,128)(2,1)S(1)}, s32[1]{0:T(128)}, s32[1]{0:T(128)}, f32[1,128]{1,0:T(1,128)}) custom-call(bf16[256,1024]{1,0:T(8,128)(2,1)} %tokens_hbm.1, s32[1,256]{1,0:T(1,128)} %bitcast.13, s32[1,128]{1,0:T(1,128)} %source_hbm.1, s32[1,128]{1,0:T(1,128)} %target_hbm.1, s32[1]{0:T(128)S(6)} %copy.21.count_ref, ...), custom_call_target="tpu_custom_call" | custom-call | flops 1000000000 | bytes 4194304 | tf_op jit(solution)/shard_map/pallas_call | solution.py:750
  37.0 59.3 %conditional.2 = (s32[1]{0:T(128)}, bf16[256,1024]{1,0:T(8,128)(2,1)S(1)}) conditional(s32[]{:T(128)} %bitcast.2, (s32[1]{0:T(128)}, bf16[256,1024]{1,0:T(8,128)(2,1)S(1)}, bf16[16,128]{1,0:T(8,128)(2,1)S(1)}, f32[1,1024]{1,0:T(1,128)}, f32[1,1024]{1,0:T(1,128)}, /*index=5*/bf16[3,1024,512]{2,1,0:T(8,128)(2,1)}, bf16[512,1024]{1,0:T(8,128)(2,1)}, ...), branch_computations={%region_0.0_spmd, %region_1.0_spmd} | conditional | flops 8589934592 | bytes 16777232 | solution.py:824
  37.0 59.1 %branch_0_fun.2 = (bf16[256,1024]{1,0:T(8,128)(2,1)S(1)}, s32[1]{0:T(128)}) custom-call(s32[1]{0:T(128)} %get-tuple-element.63.total_ref, bf16[256,1024]{1,0:T(8,128)(2,1)S(1)} %get-tuple-element.64.balanced_ref, bf16[16,128]{1,0:T(8,128)(2,1)S(1)} %get-tuple-element.65.bias_ref, f32[1,1024]{1,0:T(1,128)} %get-tuple-element.66.attn_gain_ref, ...), custom_call_target="tpu_custom_call" | custom-call | flops 5670699008 | bytes 16777216 | tf_op jit(solution)/shard_map/cond/branch_0_fun/pallas_call | solution.py:410
  96.9 0.0 copy-start
  96.9 83.9 %conditional.3 = (bf16[256,1024]{1,0:T(8,128)(2,1)S(1)}) conditional(s32[]{:T(128)} %bitcast.4, (s32[1]{0:T(128)}, bf16[256,1024]{1,0:T(8,128)(2,1)S(1)}, bf16[16,128]{1,0:T(8,128)(2,1)S(1)}, f32[1,1024]{1,0:T(1,128)}, f32[1,1024]{1,0:T(1,128)}, /*index=5*/bf16[3,1024,512]{2,1,0:T(8,128)(2,1)}, bf16[512,1024]{1,0:T(8,128)(2,1)}, ...), branch_computations={%region_2.0_spmd, %region_3.0_spmd} | conditional | flops 8589934592 | bytes 16777224 | solution.py:827
  97.2 83.6 %branch_0_fun.3 = (bf16[256,1024]{1,0:T(8,128)(2,1)S(1)}, s32[1]{0:T(128)}) custom-call(s32[1]{0:T(128)} %get-tuple-element.85.total_ref, bf16[256,1024]{1,0:T(8,128)(2,1)S(1)} %get-tuple-element.86.balanced_ref, bf16[16,128]{1,0:T(8,128)(2,1)S(1)} %get-tuple-element.87.bias_ref, f32[1,1024]{1,0:T(1,128)} %get-tuple-element.88.attn_gain_ref, ...), custom_call_target="tpu_custom_call" | custom-call | flops 8589934592 | bytes 16777216 | tf_op jit(solution)/shard_map/cond/branch_0_fun/pallas_call | solution.py:410
  180.8 0.8 copy.22
  181.6 0.0 copy-done
  181.6 0.5 copy.23
Async XLA Ops:
  96.9 84.7 %copy-start = (f32[1,128]{1,0:T(1,128)S(1)}, f32[1,128]{1,0:T(1,128)}, u32[]{:S(2)}) copy-start(f32[1,128]{1,0:T(1,128)} %get-tuple-element.110) | copy-start | bytes 1540

commit v6 on v5

--- a/solution.py
+++ b/solution.py
@@ -258,6 +258,34 @@
     zero = jnp.zeros((), jnp.bfloat16)
     value_head = (lane == 0).astype(jnp.bfloat16)
 
+    def back(mask):
+        return pltpu.make_async_remote_copy(
+            o_send.at[mask], o_buf.at[cube_index()], back_send.at[mask], back_recv.at[mask],
+            device_id=(far(mask), core), device_id_type=MESH,
+        )
+
+    def back_in(mask):
+        return pltpu.make_async_remote_copy(
+            o_send.at[mask], o_buf.at[cube_index(mask)], back_send.at[mask], back_recv.at[mask],
+            device_id=(far(mask), core), device_id_type=MESH,
+        )
+
+    own_o = pltpu.make_async_copy(o_send.at[0], o_buf.at[cube_index()], local_sem.at[2])
+    early = cut // rows
+
+    def finish(start, stop):
+        begin = start * rows // LANES * LANES
+        end = cut if stop == early else queries
+        scaled = (acc[:, begin:end] / acc[:1, begin:end]).T.astype(jnp.bfloat16)
+        for a in range(start, stop):
+            at = a * rows - begin
+            first = scaled[at : at + upper, HEAD_DIM:]
+            other = scaled[at + upper : at + rows, HEAD_DIM:]
+            if lower < upper:
+                other = jnp.concatenate([other, jnp.zeros((upper - lower, HEAD_DIM), jnp.bfloat16)], axis=0)
+            o_send[a] = jnp.concatenate([first, other], axis=1)
+            (back(a) if a else own_o).start()
+
     def step(i, carry):
         for place in CAME:
 
@@ -288,33 +316,17 @@
             else:
                 p = jnp.exp2(s).astype(jnp.bfloat16)
                 acc[:, begin:end] += dot32(v2[...], p, TN)
+            if end == cut:
+
+                @pl.when(i == 7)
+                def _():
+                    finish(0, early)
+
         return carry
 
     lax.fori_loop(0, 8, step, 0)
 
-    def back(mask):
-        return pltpu.make_async_remote_copy(
-            o_send.at[mask], o_buf.at[cube_index()], back_send.at[mask], back_recv.at[mask],
-            device_id=(far(mask), core), device_id_type=MESH,
-        )
-
-    def back_in(mask):
-        return pltpu.make_async_remote_copy(
-            o_send.at[mask], o_buf.at[cube_index(mask)], back_send.at[mask], back_recv.at[mask],
-            device_id=(far(mask), core), device_id_type=MESH,
-        )
-
-    scaled = (acc[...] / acc[:1, :]).T.astype(jnp.bfloat16)
-    for a in range(heads):
-        first = scaled[a * rows : a * rows + upper, HEAD_DIM:]
-        other = scaled[a * rows + upper : (a + 1) * rows, HEAD_DIM:]
-        if lower < upper:
-            other = jnp.concatenate([other, jnp.zeros((upper - lower, HEAD_DIM), jnp.bfloat16)], axis=0)
-        o_send[a] = jnp.concatenate([first, other], axis=1)
-    for mask in range(1, 8):
-        back(mask).start()
-    own_o = pltpu.make_async_copy(o_send.at[0], o_buf.at[cube_index()], local_sem.at[2])
-    own_o.start()
+    finish(early, heads)
     weight_copies[1].wait()
     own_o.wait()
     for mask in range(1, 8):

time: 182 us -> 184 us (1.011)
  no operation moved by 1% of the time
where the time goes in v6:
time: 184 us
  Pallas kernels  179 us (97%)
  between operations  2.55 us (1%)
    pallas_call x2, Pallas kernels, layer(): pl.pallas_call(functools.partial(layer_kernel, rows, 64 * (total_rows - r...  144 us
    pallas_call x1, Pallas kernels, deal(): pl.pallas_call(functools.partial(deal_kernel, choices), in_specs=[hbm, hb...  35.1 us

profile of v6, /device:TPU:1, one launch (start us, length us, event | category | flops | bytes accessed | tf_op | source)
XLA Modules:
  0.0 183.5 jit_solution(491050769968476997)
XLA Ops:
  1.3 35.1 %shard_map.122 = (bf16[256,1024]{1,0:T(8,128)(2,1)S(1)}, bf16[16,128]{1,0:T(8,128)(2,1)S(1)}, s32[1]{0:T(128)}, s32[1]{0:T(128)}, f32[1,128]{1,0:T(1,128)}) custom-call(bf16[256,1024]{1,0:T(8,128)(2,1)} %tokens_hbm.1, s32[1,256]{1,0:T(1,128)} %bitcast.13, s32[1,128]{1,0:T(1,128)} %source_hbm.1, s32[1,128]{1,0:T(1,128)} %target_hbm.1, s32[1]{0:T(128)S(6)} %copy.21.count_ref, ...), custom_call_target="tpu_custom_call" | custom-call | flops 1000000000 | bytes 4194304 | tf_op jit(solution)/shard_map/pallas_call | solution.py:762
  37.0 59.9 %conditional.2 = (s32[1]{0:T(128)}, bf16[256,1024]{1,0:T(8,128)(2,1)S(1)}) conditional(s32[]{:T(128)} %bitcast.2, (s32[1]{0:T(128)}, bf16[256,1024]{1,0:T(8,128)(2,1)S(1)}, bf16[16,128]{1,0:T(8,128)(2,1)S(1)}, f32[1,1024]{1,0:T(1,128)}, f32[1,1024]{1,0:T(1,128)}, /*index=5*/bf16[3,1024,512]{2,1,0:T(8,128)(2,1)}, bf16[512,1024]{1,0:T(8,128)(2,1)}, ...), branch_computations={%region_0.0_spmd, %region_1.0_spmd} | conditional | flops 8589934592 | bytes 16777232 | solution.py:836
  37.0 59.7 %branch_0_fun.2 = (bf16[256,1024]{1,0:T(8,128)(2,1)S(1)}, s32[1]{0:T(128)}) custom-call(s32[1]{0:T(128)} %get-tuple-element.63.total_ref, bf16[256,1024]{1,0:T(8,128)(2,1)S(1)} %get-tuple-element.64.balanced_ref, bf16[16,128]{1,0:T(8,128)(2,1)S(1)} %get-tuple-element.65.bias_ref, f32[1,1024]{1,0:T(1,128)} %get-tuple-element.66.attn_gain_ref, ...), custom_call_target="tpu_custom_call" | custom-call | flops 5670699008 | bytes 16777216 | tf_op jit(solution)/shard_map/cond/branch_0_fun/pallas_call | solution.py:422
  97.5 0.0 copy-start
  97.5 84.7 %conditional.3 = (bf16[256,1024]{1,0:T(8,128)(2,1)S(1)}) conditional(s32[]{:T(128)} %bitcast.4, (s32[1]{0:T(128)}, bf16[256,1024]{1,0:T(8,128)(2,1)S(1)}, bf16[16,128]{1,0:T(8,128)(2,1)S(1)}, f32[1,1024]{1,0:T(1,128)}, f32[1,1024]{1,0:T(1,128)}, /*index=5*/bf16[3,1024,512]{2,1,0:T(8,128)(2,1)}, bf16[512,1024]{1,0:T(8,128)(2,1)}, ...), branch_computations={%region_2.0_spmd, %region_3.0_spmd} | conditional | flops 8589934592 | bytes 16777224 | solution.py:839
  97.8 84.4 %branch_0_fun.3 = (bf16[256,1024]{1,0:T(8,128)(2,1)S(1)}, s32[1]{0:T(128)}) custom-call(s32[1]{0:T(128)} %get-tuple-element.85.total_ref, bf16[256,1024]{1,0:T(8,128)(2,1)S(1)} %get-tuple-element.86.balanced_ref, bf16[16,128]{1,0:T(8,128)(2,1)S(1)} %get-tuple-element.87.bias_ref, f32[1,1024]{1,0:T(1,128)} %get-tuple-element.88.attn_gain_ref, ...), custom_call_target="tpu_custom_call" | custom-call | flops 8589934592 | bytes 16777216 | tf_op jit(solution)/shard_map/cond/branch_0_fun/pallas_call | solution.py:422
  182.2 0.8 copy.22
  183.0 0.0 copy-done
  183.0 0.5 copy.23
Async XLA Ops:
  97.5 85.5 %copy-start = (f32[1,128]{1,0:T(1,128)S(1)}, f32[1,128]{1,0:T(1,128)}, u32[]{:S(2)}) copy-start(f32[1,128]{1,0:T(1,128)} %get-tuple-element.110) | copy-start | bytes 1540
